TPU v7x, 32 devices: a whole 2x2x4 slice. The times are simulated.
32 devices in a mesh: dp: 4 (over y, x), seq: 8 (over z, core).
Axes of the slice: x: 2, y: 2, z: 4, core: 2. Of those that a mesh axis runs over, the one named last changes fastest.
Arguments:
- hidden_in: bfloat16 [8, 1024, 768], P('dp', 'seq'), may hold values from -6 to 6
- lengths: int32 [8], P('dp'), may hold values from 1 to 1024, as said below
- w_attn_in: bfloat16 [2, 768, 2304], P(None, ('dp', 'seq')), may hold values from -0.21875 to 0.21875
- w_attn_out: bfloat16 [2, 768, 768], P(None, ('dp', 'seq')), may hold values from -0.875 to 0.875
- w_up: bfloat16 [2, 768, 3072], P(None, ('dp', 'seq')), may hold values from -0.21875 to 0.21875
- w_down: bfloat16 [2, 3072, 768], P(None, ('dp', 'seq')), may hold values from -0.109375 to 0.109375
- gains: bfloat16 [2, 2, 768], P(None, None, ('dp', 'seq')), may hold values from 0.25 to 1.75
- biases: bfloat16 [2, 6, 768], P(None, None, ('dp', 'seq')), may hold values from -3 to 3
- bias_hidden: bfloat16 [2, 3072], P(None, ('dp', 'seq')), may hold values from -3 to 3
- grad_out: bfloat16 [8, 1024, 768], P('dp', 'seq'), may hold values from -6 to 6
Outputs:
- hidden_out: bfloat16 [8, 1024, 768], P('dp', 'seq')
- grad_in: bfloat16 [8, 1024, 768], P('dp', 'seq')
- grad_attn_in: float32 [2, 768, 2304], P(None, ('dp', 'seq'))
- grad_attn_out: float32 [2, 768, 768], P(None, ('dp', 'seq'))
- grad_up: float32 [2, 768, 3072], P(None, ('dp', 'seq'))
- grad_down: float32 [2, 3072, 768], P(None, ('dp', 'seq'))
- grad_gains: float32 [2, 2, 768], P(None, None, ('dp', 'seq'))
- grad_biases: float32 [2, 6, 768], P(None, None, ('dp', 'seq'))
- grad_bias_hidden: float32 [2, 3072], P(None, ('dp', 'seq'))
Inputs may be any that keep to these rules, and one draw needn't show every extreme that they name: `lengths`: in each group of 2 consecutive slots (one index of dp) one sequence has exactly 1024 tokens.
All inputs are finite; a program needn't handle non-finite values.
Results may differ from a plain program's by a relative error of at most 0.03.
Values may be sent and summed in bfloat16 or wider, within the bound.
A program may use at most 256 MiB of HBM per device.

v0:
```python
import math

import jax
import jax.numpy as jnp
from jax import lax
from jax.sharding import PartitionSpec as P

D = 768
HEADS = 12
HEAD_DIM = 64
LAYERS = 2


EPSILON = 1e-12
MASKED = -1000000000.0


def layer_norm(summed, gain, shift):
    center = jnp.mean(summed, axis=-1, keepdims=True)
    offset = summed - center
    spread = jnp.mean(offset * offset, axis=-1, keepdims=True)
    return offset * lax.rsqrt(spread + EPSILON) * gain + shift


def norm_back(summed, gain, shift, upstream):
    _, pull = jax.vjp(layer_norm, summed, gain, shift)
    return pull(upstream)


def gelu_back(hidden, upstream):
    _, pull = jax.vjp(lambda inner: jax.nn.gelu(inner, approximate=False), hidden)
    return pull(upstream)[0]


def heads_of(array):
    return array.reshape(array.shape[0], array.shape[1], HEADS, HEAD_DIM)


def window(array, start, step):
    return lax.dynamic_slice_in_dim(array, start, step, 1)


def scores_for(query_heads, keys_part, live_part):
    scale = 1.0 / math.sqrt(HEAD_DIM)
    raw = (
        jnp.einsum(
            "sqhe,skhe->shqk", query_heads, heads_of(keys_part), preferred_element_type=jnp.float32
        )
        * scale
    )
    return jnp.where(live_part[:, None, None, :], raw, MASKED)


def attend(query, keys_all, values_all, live_keys):
    seqs, block, width = query.shape
    span = keys_all.shape[1]
    step = math.gcd(span, 512)
    query_heads = heads_of(query)

    def add_stats(state, index):
        peak, total = state
        scores = scores_for(
            query_heads, window(keys_all, index * step, step), window(live_keys, index * step, step)
        )
        higher = jnp.maximum(peak, jnp.max(scores, axis=-1))
        total = total * jnp.exp(peak - higher) + jnp.sum(
            jnp.exp(scores - higher[..., None]), axis=-1
        )
        return ((higher, total), None)

    start_peak = jnp.full((seqs, HEADS, block), MASKED, jnp.float32)
    (peak, total), _ = lax.scan(
        add_stats, (start_peak, jnp.zeros_like(start_peak)), jnp.arange(span // step)
    )
    log_total = peak + jnp.log(total)

    def add_values(state, index):
        scores = scores_for(
            query_heads, window(keys_all, index * step, step), window(live_keys, index * step, step)
        )
        probs = jnp.exp(scores - log_total[..., None]).astype(jnp.bfloat16)
        values_part = heads_of(window(values_all, index * step, step))
        return (
            state
            + jnp.einsum("shqk,skhe->sqhe", probs, values_part, preferred_element_type=jnp.float32),
            None,
        )

    mixed, _ = lax.scan(
        add_values, jnp.zeros((seqs, block, HEADS, HEAD_DIM), jnp.float32), jnp.arange(span // step)
    )
    return (log_total, mixed.reshape(seqs, block, width))


def query_grads(query, keys_all, values_all, live_keys, log_total, mixed_grad, delta):
    seqs, block, width = query.shape
    span = keys_all.shape[1]
    step = math.gcd(span, 512)
    query_heads = heads_of(query)
    upstream_heads = heads_of(mixed_grad)

    def add_block(state, index):
        keys_part = window(keys_all, index * step, step)
        scores = scores_for(query_heads, keys_part, window(live_keys, index * step, step))
        probs = jnp.exp(scores - log_total[..., None])
        values_part = heads_of(window(values_all, index * step, step))
        grad_probs = jnp.einsum(
            "sqhe,skhe->shqk", upstream_heads, values_part, preferred_element_type=jnp.float32
        )
        grad_scores = (probs * (grad_probs - delta[..., None])).astype(jnp.bfloat16)
        return (
            state
            + jnp.einsum(
                "shqk,skhe->sqhe",
                grad_scores,
                heads_of(keys_part),
                preferred_element_type=jnp.float32,
            ),
            None,
        )

    summed, _ = lax.scan(
        add_block, jnp.zeros((seqs, block, HEADS, HEAD_DIM), jnp.float32), jnp.arange(span // step)
    )
    return (summed * (1.0 / math.sqrt(HEAD_DIM))).reshape(seqs, block, width).astype(jnp.bfloat16)


def forward_layer(state, weights, live_keys):
    w_in, w_out, w_hid, w_back, gain, bias, bias_h = weights
    gain = gain.astype(jnp.float32)
    bias = bias.astype(jnp.float32)
    bias_h = bias_h.astype(jnp.float32)
    lowered = state.astype(jnp.bfloat16)
    projected = jnp.dot(lowered, w_in, preferred_element_type=jnp.float32)
    query = (projected[..., :D] + bias[0]).astype(jnp.bfloat16)
    key = projected[..., D : 2 * D].astype(jnp.bfloat16)
    value = (projected[..., 2 * D :] + bias[1]).astype(jnp.bfloat16)
    keys_all, values_all = (
        lax.all_gather(key, "seq", axis=1, tiled=True),
        lax.all_gather(value, "seq", axis=1, tiled=True),
    )
    log_total, mixed_full = attend(query, keys_all, values_all, live_keys)
    mixed = mixed_full.astype(jnp.bfloat16)
    first_sum = state + (jnp.dot(mixed, w_out, preferred_element_type=jnp.float32) + bias[2])
    normed = layer_norm(first_sum, gain[0], bias[4])
    normed_low = normed.astype(jnp.bfloat16)
    hidden = jnp.dot(normed_low, w_hid, preferred_element_type=jnp.float32) + bias_h
    activated = jax.nn.gelu(hidden, approximate=False).astype(jnp.bfloat16)
    second_sum = normed + (jnp.dot(activated, w_back, preferred_element_type=jnp.float32) + bias[3])
    result = layer_norm(second_sum, gain[1], bias[5])
    saved = (
        lowered,
        query,
        key,
        value,
        None,
        log_total,
        mixed_full,
        mixed,
        first_sum,
        normed_low,
        hidden,
        activated,
        second_sum,
    )
    return (result, saved)


def backward_layer(upstream, weights, saved, live_keys, block):
    w_in, w_out, w_hid, w_back, gain, bias, bias_h = weights
    gain = gain.astype(jnp.float32)
    bias = bias.astype(jnp.float32)
    (
        lowered,
        query,
        key,
        value,
        kept_pair,
        log_total,
        mixed_full,
        mixed,
        first_sum,
        normed_low,
        hidden,
        activated,
        second_sum,
    ) = saved
    seqs, rows, width = query.shape
    keys_all, values_all = (
        lax.all_gather(key, "seq", axis=1, tiled=True),
        lax.all_gather(value, "seq", axis=1, tiled=True),
    )
    grad_second, grad_gain_two, grad_shift_two = norm_back(second_sum, gain[1], bias[5], upstream)
    down_grad = grad_second.astype(jnp.bfloat16)
    grad_bias_down = jnp.sum(grad_second, axis=(0, 1))
    grad_down_w = jnp.einsum(
        "sqf,sqd->fd", activated, down_grad, preferred_element_type=jnp.float32
    )
    grad_activated = jnp.einsum(
        "sqd,fd->sqf", down_grad, w_back, preferred_element_type=jnp.float32
    )
    hidden_grad = gelu_back(hidden, grad_activated).astype(jnp.bfloat16)
    grad_bias_h = jnp.sum(hidden_grad.astype(jnp.float32), axis=(0, 1))
    grad_up_w = jnp.einsum(
        "sqd,sqf->df", normed_low, hidden_grad, preferred_element_type=jnp.float32
    )
    grad_normed = grad_second + jnp.einsum(
        "sqf,df->sqd", hidden_grad, w_hid, preferred_element_type=jnp.float32
    )
    grad_first, grad_gain_one, grad_shift_one = norm_back(first_sum, gain[0], bias[4], grad_normed)
    out_grad = grad_first.astype(jnp.bfloat16)
    grad_bias_out = jnp.sum(grad_first, axis=(0, 1))
    grad_out_w = jnp.einsum("sqd,sqe->de", mixed, out_grad, preferred_element_type=jnp.float32)
    mixed_grad = jnp.einsum(
        "sqe,de->sqd", out_grad, w_out, preferred_element_type=jnp.float32
    ).astype(jnp.bfloat16)
    delta = jnp.sum(heads_of(mixed_grad.astype(jnp.float32) * mixed_full), axis=-1).transpose(
        0, 2, 1
    )
    query_grad = query_grads(query, keys_all, values_all, live_keys, log_total, mixed_grad, delta)
    query_heads = heads_of(query)
    upstream_heads = heads_of(mixed_grad)
    scale = 1.0 / math.sqrt(HEAD_DIM)
    step = math.gcd(block * lax.axis_size("seq"), 512)

    def one_block(index):
        start = index * step
        keys_part = window(keys_all, start, step)
        values_part = heads_of(window(values_all, start, step))
        scores = scores_for(query_heads, keys_part, window(live_keys, start, step))
        probs = jnp.exp(scores - log_total[..., None])
        grad_probs = jnp.einsum(
            "sqhe,skhe->shqk", upstream_heads, values_part, preferred_element_type=jnp.float32
        )
        grad_scores = (probs * (grad_probs - delta[..., None])).astype(jnp.bfloat16)
        grad_keys = (
            jnp.einsum(
                "shqk,sqhe->kshe", grad_scores, query_heads, preferred_element_type=jnp.float32
            )
            * scale
        )
        grad_values = jnp.einsum(
            "shqk,sqhe->kshe",
            probs.astype(jnp.bfloat16),
            upstream_heads,
            preferred_element_type=jnp.float32,
        )
        return jnp.concatenate(
            (grad_keys.reshape(step, seqs, width), grad_values.reshape(step, seqs, width)), axis=-1
        )

    pieces = lax.map(one_block, jnp.arange(block * lax.axis_size("seq") // step))
    shares = lax.psum_scatter(
        pieces.reshape(block * lax.axis_size("seq"), seqs, 2 * width).astype(jnp.bfloat16),
        "seq",
        scatter_dimension=0,
        tiled=True,
    ).astype(jnp.float32)
    key_grad = shares[..., :width].transpose(1, 0, 2).astype(jnp.bfloat16)
    value_grad = shares[..., width:].transpose(1, 0, 2).astype(jnp.bfloat16)
    projected_grad = jnp.concatenate((query_grad, key_grad, value_grad), axis=-1)
    grad_bias_query = jnp.sum(query_grad.astype(jnp.float32), axis=(0, 1))
    grad_bias_value = jnp.sum(value_grad.astype(jnp.float32), axis=(0, 1))
    grad_in_w = jnp.einsum(
        "sqd,sqe->de", lowered, projected_grad, preferred_element_type=jnp.float32
    )
    grad_state = grad_first + jnp.einsum(
        "sqe,de->sqd", projected_grad, w_in, preferred_element_type=jnp.float32
    )
    grad_gains_now = jnp.stack([grad_gain_one, grad_gain_two])
    grad_biases_now = jnp.stack(
        [
            grad_bias_query,
            grad_bias_value,
            grad_bias_out,
            grad_bias_down,
            grad_shift_one,
            grad_shift_two,
        ]
    )
    terms = (
        grad_in_w,
        grad_out_w,
        grad_up_w,
        grad_down_w,
        grad_gains_now,
        grad_biases_now,
        grad_bias_h,
    )
    return (grad_state, terms)


def per_device(
    hidden_in, lengths, w_attn_in, w_attn_out, w_up, w_down, gains, biases, bias_hidden, grad_out
):
    seqs, block, width = hidden_in.shape
    span = block * lax.axis_size("seq")
    first_row = lax.axis_index("seq") * block
    live_keys = jnp.arange(span, dtype=jnp.int32)[None, :] < lengths[:, None]
    live_rows = (
        (first_row + jnp.arange(block, dtype=jnp.int32))[None, :] < lengths[:, None]
    ).astype(jnp.float32)
    state = hidden_in.astype(jnp.float32)
    stored = []
    for layer in range(LAYERS):
        weights = (
            lax.all_gather(w_attn_in[layer], ("dp", "seq"), axis=0, tiled=True),
            lax.all_gather(w_attn_out[layer], ("dp", "seq"), axis=0, tiled=True),
            lax.all_gather(w_up[layer], ("dp", "seq"), axis=0, tiled=True),
            lax.all_gather(w_down[layer], ("dp", "seq"), axis=0, tiled=True),
            lax.all_gather(gains[layer], ("dp", "seq"), axis=1, tiled=True),
            lax.all_gather(biases[layer], ("dp", "seq"), axis=1, tiled=True),
            lax.all_gather(bias_hidden[layer], ("dp", "seq"), axis=0, tiled=True),
        )
        state, saved = forward_layer(state, weights, live_keys)
        stored.append((None, saved))
    upstream = grad_out.astype(jnp.float32) * live_rows[..., None]
    collected = []
    for layer in reversed(range(LAYERS)):
        weights, saved = stored[layer]
        weights = (
            lax.all_gather(w_attn_in[layer], ("dp", "seq"), axis=0, tiled=True),
            lax.all_gather(w_attn_out[layer], ("dp", "seq"), axis=0, tiled=True),
            lax.all_gather(w_up[layer], ("dp", "seq"), axis=0, tiled=True),
            lax.all_gather(w_down[layer], ("dp", "seq"), axis=0, tiled=True),
            lax.all_gather(gains[layer], ("dp", "seq"), axis=1, tiled=True),
            lax.all_gather(biases[layer], ("dp", "seq"), axis=1, tiled=True),
            lax.all_gather(bias_hidden[layer], ("dp", "seq"), axis=0, tiled=True),
        )
        upstream, terms = backward_layer(upstream, weights, saved, live_keys, block)
        collected.insert(
            0,
            (
                lax.psum_scatter(terms[0], ("dp", "seq"), scatter_dimension=0, tiled=True),
                lax.psum_scatter(terms[1], ("dp", "seq"), scatter_dimension=0, tiled=True),
                lax.psum_scatter(terms[2], ("dp", "seq"), scatter_dimension=0, tiled=True),
                lax.psum_scatter(terms[3], ("dp", "seq"), scatter_dimension=0, tiled=True),
                lax.psum_scatter(terms[4], ("dp", "seq"), scatter_dimension=1, tiled=True),
                lax.psum_scatter(terms[5], ("dp", "seq"), scatter_dimension=1, tiled=True),
                lax.psum_scatter(terms[6], ("dp", "seq"), scatter_dimension=0, tiled=True),
            ),
        )
    stacked = tuple((jnp.stack([shares[member] for shares in collected]) for member in range(7)))
    return (state.astype(jnp.bfloat16), upstream.astype(jnp.bfloat16)) + stacked


def solution(mesh):
    placed = (
        P("dp", "seq", None),
        P("dp"),
        P(None, ("dp", "seq"), None),
        P(None, ("dp", "seq"), None),
        P(None, ("dp", "seq"), None),
        P(None, ("dp", "seq"), None),
        P(None, None, ("dp", "seq")),
        P(None, None, ("dp", "seq")),
        P(None, ("dp", "seq")),
        P("dp", "seq", None),
    )
    return jax.shard_map(
        per_device,
        mesh=mesh,
        in_specs=placed,
        out_specs=(
            P("dp", "seq", None),
            P("dp", "seq", None),
            P(None, ("dp", "seq"), None),
            P(None, ("dp", "seq"), None),
            P(None, ("dp", "seq"), None),
            P(None, ("dp", "seq"), None),
            P(None, None, ("dp", "seq")),
            P(None, None, ("dp", "seq")),
            P(None, ("dp", "seq")),
        ),
        check_vma=False,
    )
```

profile of v0, /device:TPU:0, one launch (start us, length us, event | category | flops | bytes accessed | tf_op | source)
XLA Modules:
  0.0 2162.7 jit_solution(6961832292475723949)
XLA Ops:
  9.0 65.6 %all-gather.35.cloned.1.call-done = bf16[1,768,2304]{2,1,0:T(8,128)(2,1)} async-done(((bf16[1,24,2304]{2,1,0:T(8,128)(2,1)}), bf16[1,768,2304]{2,1,0:T(8,128)(2,1)}) %all-gather.35.cloned.1.call-update) | async-done | bytes 3538960 | tf_op jit(solution)/shard_map/all_gather | solution.py:307
  79.4 43.5 %all-gather.1 = bf16[1,6,768]{1,0,2:T(2,128)(2,1)S(1)} all-gather(bf16[1,6,24]{1,0,2:T(2,128)(2,1)S(1)} %copy.198), channel_id=3, replica_groups=mesh['dp'=4,'seq'=8] {'dp','seq'}, dimensions={2}, use_global_device_ids=true | all-gather | bytes 9504 | tf_op jit(solution)/shard_map/all_gather | solution.py:312
  142.0 39.2 %all-reduce.9 = (bf16[3072]{0:T(1024)(128)(2,1)}, bf16[3072]{0:T(1024)(128)(2,1)S(1)}) all-reduce(bf16[3072]{0:T(1024)(128)(2,1)S(1)} %dynamic-update-slice.1, bf16[3072]{0:T(1024)(128)(2,1)S(1)} %dynamic-update-slice), channel_id=14, replica_groups=mesh['dp'=4,'seq'=8] {'dp','seq'}, use_global_device_ids=true, to_apply=%add.1 | all-reduce | flops 6144 | bytes 24576
  182.4 43.8 %all-gather.3 = bf16[1,2,768]{1,0,2:T(2,128)(2,1)S(1)} all-gather(bf16[1,2,24]{1,0,2:T(2,128)(2,1)S(1)} %copy.199), channel_id=5, replica_groups=mesh['dp'=4,'seq'=8] {'dp','seq'}, dimensions={2}, use_global_device_ids=true | all-gather | bytes 3168 | tf_op jit(solution)/shard_map/all_gather | solution.py:311
  320.7 41.1 %all-gather.41.cloned.1.call-done = bf16[1,3072,768]{2,1,0:T(8,128)(2,1)} async-done(((bf16[1,96,768]{2,1,0:T(8,128)(2,1)}), bf16[1,3072,768]{2,1,0:T(8,128)(2,1)}) %all-gather.41.cloned.1.call-update) | async-done | bytes 4718608 | tf_op jit(solution)/shard_map/all_gather | solution.py:310
  366.0 58.0 %all-gather.43.cloned.1.call-done = bf16[1,768,2304]{2,1,0:T(8,128)(2,1)} async-done(((bf16[1,24,2304]{2,1,0:T(8,128)(2,1)}), bf16[1,768,2304]{2,1,0:T(8,128)(2,1)}) %all-gather.43.cloned.1.call-update) | async-done | bytes 3538960 | tf_op jit(solution)/shard_map/all_gather | solution.py:307
  428.1 43.6 %all-gather.8 = bf16[1,6,768]{1,0,2:T(2,128)(2,1)S(1)} all-gather(bf16[1,6,24]{1,0,2:T(2,128)(2,1)S(1)} %copy.200), channel_id=10, replica_groups=mesh['dp'=4,'seq'=8] {'dp','seq'}, dimensions={2}, use_global_device_ids=true | all-gather | bytes 9504 | tf_op jit(solution)/shard_map/all_gather | solution.py:312
  488.5 40.3 %all-gather.10 = bf16[1,2,768]{1,0,2:T(2,128)(2,1)S(1)} all-gather(bf16[1,2,24]{1,0,2:T(2,128)(2,1)S(1)} %copy.201), channel_id=12, replica_groups=mesh['dp'=4,'seq'=8] {'dp','seq'}, dimensions={2}, use_global_device_ids=true | all-gather | bytes 3168 | tf_op jit(solution)/shard_map/all_gather | solution.py:311
  598.3 49.0 %all-gather.47.cloned.1.call-done = bf16[1,768,3072]{2,1,0:T(8,128)(2,1)} async-done(((bf16[1,24,3072]{2,1,0:T(8,128)(2,1)}), bf16[1,768,3072]{2,1,0:T(8,128)(2,1)}) %all-gather.47.cloned.1.call-update) | async-done | bytes 4718608 | tf_op jit(solution)/shard_map/all_gather | solution.py:309
  662.3 51.0 %all-gather.49.cloned.1.call-done = bf16[1,3072,768]{2,1,0:T(8,128)(2,1)} async-done(((bf16[1,96,768]{2,1,0:T(8,128)(2,1)}), bf16[1,3072,768]{2,1,0:T(8,128)(2,1)}) %all-gather.49.cloned.1.call-update) | async-done | bytes 4718608 | tf_op jit(solution)/shard_map/all_gather | solution.py:310
  737.6 44.5 %while.90 = (s32[]{:T(128)}, bf16[2,512,2,1536]{1,3,2,0:T(8,128)(2,1)}, s32[2]{0:T(128)S(1)}, pred[2,1024]{1,0:T(4,128)(4,1)S(1)}, bf16[2,1024,768]{1,2,0:T(8,12...) while((s32[]{:T(128)}, ...), condition=%wide.region_28.29_spmd, body=%wide.region_27.28_spmd.sunk | while | flops 828899328 | bytes 45654752 | solution.py:252
  793.1 31.7 %while.96 = (s32[]{:T(128)}, f32[2,128,12,64]{1,3,2,0:T(8,128)}, s32[2]{0:T(128)S(1)}, bf16[2,1024,768]{1,2,0:T(8,128)(2,1)S(1)}, pred[2,1024]{1,0:T(4,128)(4,1)...) while((s32[]{:T(128)}, f32[2,128,12,64]{1,3,2,0:T(8,128)}, ...), condition=%wide.region_26.27_spmd.clone, body=%wide.region_25.26_spmd.clone.sunk | while | flops 613810176 | bytes 25980140 | solution.py:122
  827.1 32.5 %reduce-scatter.19.cloned.1.call-done = bf16[128,2,1536]{2,0,1:T(8,128)(2,1)} async-done(((bf16[1024,2,1536]{2,0,1:T(8,128)(2,1)}), bf16[128,2,1536]{2,0,1:T(8,128)(2,1)}) %reduce-scatter.19.cloned.1.call-update) | async-done | bytes 786448 | tf_op jit(solution)/shard_map/reduce_scatter | solution.py:253
  880.3 44.6 %while.91 = (s32[]{:T(128)}, bf16[2,512,2,1536]{1,3,2,0:T(8,128)(2,1)}, s32[2]{0:T(128)S(1)}, pred[2,1024]{1,0:T(4,128)(4,1)S(1)}, bf16[2,1024,768]{1,2,0:T(8,12...) while((s32[]{:T(128)}, ...), condition=%wide.region_38.39_spmd, body=%wide.region_37.38_spmd.sunk | while | flops 828899328 | bytes 45654872 | solution.py:252
  990.1 32.6 %while.97 = (s32[]{:T(128)}, f32[2,128,12,64]{1,3,2,0:T(8,128)}, s32[2]{0:T(128)}, bf16[2,1024,768]{1,2,0:T(8,128)(2,1)S(1)}, pred[2,1024]{1,0:T(4,128)(4,1)S(1)...) while((s32[]{:T(128)}, f32[2,128,12,64]{1,3,2,0:T(8,128)}, ...), condition=%wide.region_36.37_spmd.clone, body=%wide.region_35.36_spmd.clone.sunk | while | flops 613810176 | bytes 25980140 | solution.py:122
  1046.0 58.5 %reduce-scatter.25.cloned.1.call-done = f32[24,768]{1,0:T(8,128)} async-done(((f32[768,768]{1,0:T(8,128)}), f32[24,768]{1,0:T(8,128)}) %reduce-scatter.25.cloned.1.call-update) | async-done | bytes 73744 | tf_op jit(solution)/shard_map/reduce_scatter | solution.py:335
  1104.5 104.1 %reduce-scatter.23.cloned.1.call-done = f32[24,768]{1,0:T(8,128)} async-done(((f32[768,768]{1,0:T(8,128)}), f32[24,768]{1,0:T(8,128)}) %reduce-scatter.23.cloned.1.call-update) | async-done | bytes 73744 | tf_op jit(solution)/shard_map/reduce_scatter | solution.py:335
  1210.2 122.1 %reduce-scatter.37.cloned.1.call-done = f32[24,2304]{1,0:T(8,128)} async-done(((f32[768,2304]{1,0:T(8,128)}), f32[24,2304]{1,0:T(8,128)}) %reduce-scatter.37.cloned.1.call-update) | async-done | bytes 221200
  1334.0 139.8 %reduce-scatter.33.cloned.1.call-done = f32[96,768]{1,0:T(8,128)} async-done(((f32[3072,768]{1,0:T(8,128)}), f32[96,768]{1,0:T(8,128)}) %reduce-scatter.33.cloned.1.call-update) | async-done | bytes 294928 | tf_op jit(solution)/shard_map/reduce_scatter | solution.py:337
  1473.8 140.7 %reduce-scatter.31.cloned.1.call-done = f32[96,768]{1,0:T(8,128)} async-done(((f32[3072,768]{1,0:T(8,128)}), f32[96,768]{1,0:T(8,128)}) %reduce-scatter.31.cloned.1.call-update) | async-done | bytes 294928 | tf_op jit(solution)/shard_map/reduce_scatter | solution.py:337
  1616.4 139.5 %reduce-scatter.29.cloned.1.call-done = f32[24,3072]{1,0:T(8,128)} async-done(((f32[768,3072]{1,0:T(8,128)}), f32[24,3072]{1,0:T(8,128)}) %reduce-scatter.29.cloned.1.call-update) | async-done | bytes 294928 | tf_op jit(solution)/shard_map/reduce_scatter | solution.py:336
  1755.9 140.5 %reduce-scatter.27.cloned.1.call-done = f32[24,3072]{1,0:T(8,128)} async-done(((f32[768,3072]{1,0:T(8,128)}), f32[24,3072]{1,0:T(8,128)}) %reduce-scatter.27.cloned.1.call-update) | async-done | bytes 294928 | tf_op jit(solution)/shard_map/reduce_scatter | solution.py:336
  1902.2 124.3 %all-reduce.12.cloned.1.call-done = (f32[2,768]{1,0:T(2,128)}, f32[2,768]{1,0:T(2,128)}, f32[6,768]{1,0:T(8,128)}, f32[6,768]{1,0:T(8,128)}, f32[3072]{0:T(1024)}, /*index=5*/f32[3072]{0:T(1024)}) async-done(((f32[2,768]{1,0:T(2,128)}, f32[2,768]{1,0:T(2,128)}, f32[6,768]{1,0:T(8,128)}, f32[6,768]{1,0:T(8,128)}, f32[3072]{0:T(1024)}, /*index=5*/f32[3072]{0:T(1024)}), (f32[2,768]{1,0:T(2,128)}, ...) | async-done | bytes 73744
  2030.6 122.9 %reduce-scatter.35.cloned.1.call-done = f32[24,2304]{1,0:T(8,128)} async-done(((f32[768,2304]{1,0:T(8,128)}), f32[24,2304]{1,0:T(8,128)}) %reduce-scatter.35.cloned.1.call-update) | async-done | bytes 221200
  (583 shorter events, 626.3 us)
Async XLA Ops:
  7.2 67.4 %all-gather.35.cloned.1.call-start = ((), (), s32[]{:S(2)}) async-start(), calls=%async_computation.22 | async-start | bytes 3649536 | tf_op jit(solution)/shard_map/all_gather | solution.py:307
  8.9 223.1 %all-gather.29.cloned.1.call-start = ((), (), s32[]{:S(2)}) async-start(), calls=%async_computation.11 | async-start | bytes 3538944 | tf_op jit(solution)/shard_map/all_gather | solution.py:139
  78.6 182.4 %all-gather.27.cloned.1.call-start = ((), (), s32[]{:S(2)}) async-start(), calls=%async_computation.10 | async-start | bytes 3538944 | tf_op jit(solution)/shard_map/all_gather | solution.py:140
  137.7 149.3 %all-gather.37.cloned.1.call-start = ((), (), s32[]{:S(2)}) async-start(), calls=%async_computation.23 | async-start | bytes 1216512 | tf_op jit(solution)/shard_map/all_gather | solution.py:308
  138.4 158.1 %all-gather.39.cloned.1.call-start = ((), (), s32[]{:S(2)}) async-start(), calls=%async_computation.24 | async-start | bytes 4866048 | tf_op jit(solution)/shard_map/all_gather | solution.py:309
  139.2 222.7 %all-gather.41.cloned.1.call-start = ((), (), s32[]{:S(2)}) async-start(), calls=%async_computation.25 | async-start | bytes 4866048 | tf_op jit(solution)/shard_map/all_gather | solution.py:310
  140.0 283.9 %all-gather.43.cloned.1.call-start = ((), (), s32[]{:S(2)}) async-start(), calls=%async_computation.26 | async-start | bytes 3649536 | tf_op jit(solution)/shard_map/all_gather | solution.py:307
  140.8 395.1 %all-gather.33.cloned.1.call-start = ((), (), s32[]{:S(2)}) async-start(), calls=%async_computation.13 | async-start | bytes 3538944 | tf_op jit(solution)/shard_map/all_gather | solution.py:139
  428.0 111.5 %all-gather.31.cloned.1.call-start = ((), (), s32[]{:S(2)}) async-start(), calls=%async_computation.12 | async-start | bytes 3538944 | tf_op jit(solution)/shard_map/all_gather | solution.py:140
  486.5 107.2 %all-gather.45.cloned.1.call-start = ((), (), s32[]{:S(2)}) async-start(), calls=%async_computation.27 | async-start | bytes 1216512 | tf_op jit(solution)/shard_map/all_gather | solution.py:308
  487.1 160.2 %all-gather.47.cloned.1.call-start = ((), (), s32[]{:S(2)}) async-start(), calls=%async_computation.28 | async-start | bytes 4866048 | tf_op jit(solution)/shard_map/all_gather | solution.py:309
  487.8 225.4 %all-gather.49.cloned.1.call-start = ((), (), s32[]{:S(2)}) async-start(), calls=%async_computation.29 | async-start | bytes 4866048 | tf_op jit(solution)/shard_map/all_gather | solution.py:310
  488.4 371.2 %reduce-scatter.19.cloned.1.call-start = ((), (), s32[]{:S(2)}) async-start(), calls=%async_computation.14 | async-start | bytes 7077888 | tf_op jit(solution)/shard_map/reduce_scatter | solution.py:253
  790.7 239.4 %reduce-scatter.21.cloned.1.call-start = ((), (), s32[]{:S(2)}) async-start(), calls=%async_computation.15 | async-start | bytes 7077888 | tf_op jit(solution)/shard_map/reduce_scatter | solution.py:253
  933.6 170.9 %reduce-scatter.25.cloned.1.call-start = ((), (), s32[]{:S(2)}) async-start(), calls=%async_computation.17 | async-start | bytes 2433024 | tf_op jit(solution)/shard_map/reduce_scatter | solution.py:335
  937.6 271.0 %reduce-scatter.23.cloned.1.call-start = ((), (), s32[]{:S(2)}) async-start(), calls=%async_computation.16 | async-start | bytes 2433024 | tf_op jit(solution)/shard_map/reduce_scatter | solution.py:335
  941.2 391.1 %reduce-scatter.37.cloned.1.call-start = ((), (), s32[]{:S(2)}) async-start(), calls=%async_computation.31 | async-start | bytes 7299072
  946.9 526.9 %reduce-scatter.33.cloned.1.call-start = ((), (), s32[]{:S(2)}) async-start(), calls=%async_computation.21 | async-start | bytes 9732096 | tf_op jit(solution)/shard_map/reduce_scatter | solution.py:337
  954.3 660.2 %reduce-scatter.31.cloned.1.call-start = ((), (), s32[]{:S(2)}) async-start(), calls=%async_computation.20 | async-start | bytes 9732096 | tf_op jit(solution)/shard_map/reduce_scatter | solution.py:337
  961.7 794.2 %reduce-scatter.29.cloned.1.call-start = ((), (), s32[]{:S(2)}) async-start(), calls=%async_computation.19 | async-start | bytes 9732096 | tf_op jit(solution)/shard_map/reduce_scatter | solution.py:336
  969.3 927.1 %reduce-scatter.27.cloned.1.call-start = ((), (), s32[]{:S(2)}) async-start(), calls=%async_computation.18 | async-start | bytes 9732096 | tf_op jit(solution)/shard_map/reduce_scatter | solution.py:336
  976.9 1049.5 %all-reduce.12.cloned.1.call-start = ((), (), s32[]{:S(2)}) async-start(), calls=%async_computation.32 | async-start | bytes 172032
  1032.6 1120.9 %reduce-scatter.35.cloned.1.call-start = ((), (), s32[]{:S(2)}) async-start(), calls=%async_computation.30 | async-start | bytes 7299072
  1046.0 852.3 %copy-start.11 = (f32[2,128,768]{2,1,0:T(8,128)S(1)}, f32[2,128,768]{2,1,0:T(8,128)}, u32[]{:S(2)}) copy-start(f32[2,128,768]{2,1,0:T(8,128)} %copy-done.10) | copy-start | bytes 2359300
  (129 other events, 1858.7 us)
Sparse Core Ops, SparseCore 0:
  11.6 62.9 all-gather.34
  78.7 39.9 all-gather.28
  137.8 36.4 all-gather.26
  177.1 53.2 all-gather.36
  233.8 62.5 all-gather.38
  299.3 62.4 all-gather.40
  364.9 59.0 all-gather.42
  428.1 40.1 all-gather.32
  486.6 38.1 all-gather.30
  527.6 53.3 all-gather.44
  584.6 62.6 all-gather.46
  650.7 62.4 all-gather.48
  790.9 68.6 reduce-scatter.18
  933.7 68.1 reduce-scatter.20
  1007.0 97.4 reduce-scatter.24
  1110.5 98.1 reduce-scatter.22
  1214.1 118.1 reduce-scatter.36
  1339.1 134.6 reduce-scatter.32
  1479.6 134.7 reduce-scatter.30
  1621.2 134.6 reduce-scatter.28
  1761.8 134.5 reduce-scatter.26
  1904.5 121.9 all-reduce.11
  2033.1 120.3 reduce-scatter.34
where the time goes:
time: 2170 us; the launch traced here: 2160 us
  waiting for transfers between devices  1400 us (65%)
  matrix products  247 us (11%)
  blocking collectives  210 us (10%)
  local copies, waits for them, and re-layouts  194 us (9%)
  other arithmetic  85.9 us (4%)
    unnamed x26, waiting for transfers between devices  372 us
    reduce_scatter x2, waiting for transfers between devices, per_device(): lax.psum_scatter(terms[3], ('dp', 'seq'), scatter_dimension=0, tiled=True)  281 us
    reduce_scatter x2, waiting for transfers between devices, per_device(): lax.psum_scatter(terms[2], ('dp', 'seq'), scatter_dimension=0, tiled=True)  280 us
    reduce_scatter x2, waiting for transfers between devices, per_device(): lax.psum_scatter(terms[1], ('dp', 'seq'), scatter_dimension=0, tiled=True)  163 us
    all_gather x2, waiting for transfers between devices, per_device(): lax.all_gather(w_attn_in[layer], ('dp', 'seq'), axis=0, tiled=True)  124 us
    all_gather x2, waiting for transfers between devices, per_device(): lax.all_gather(w_down[layer], ('dp', 'seq'), axis=0, tiled=True)  92.1 us
    all_gather x2, blocking collectives, per_device(): lax.all_gather(biases[layer], ('dp', 'seq'), axis=1, tiled=True)  87.2 us
    all_gather x2, blocking collectives, per_device(): lax.all_gather(gains[layer], ('dp', 'seq'), axis=1, tiled=True)  84.1 us
  transfers between devices with their start and end apart: 23, of which 16 were waited for; matrix products, arithmetic and copies ran while one was open for 16% of the time, Pallas kernels for 0%

commit v1 on v0

v1 whole, which is shorter than its diff:
```python
import math

import jax
import jax.numpy as jnp
from jax import lax
from jax.sharding import PartitionSpec as P

D = 768
HEADS = 12
HEAD_DIM = 64
LAYERS = 2


EPSILON = 1e-12
MASKED = -1000000000.0


def layer_norm(summed, gain, shift):
    center = jnp.mean(summed, axis=-1, keepdims=True)
    offset = summed - center
    spread = jnp.mean(offset * offset, axis=-1, keepdims=True)
    return offset * lax.rsqrt(spread + EPSILON) * gain + shift


def norm_back(summed, gain, shift, upstream):
    _, pull = jax.vjp(layer_norm, summed, gain, shift)
    return pull(upstream)


def gelu_back(hidden, upstream):
    _, pull = jax.vjp(lambda inner: jax.nn.gelu(inner, approximate=False), hidden)
    return pull(upstream)[0]


ORDERS = {
    "in": (("seq", 1), ("dp", 2), ("dp", 1), ("seq", 2), ("seq", 4)),
    "out": (("seq", 1), ("dp", 1), ("dp", 2), ("seq", 2), ("seq", 4)),
    "up": (("seq", 1), ("dp", 1), ("seq", 2), ("dp", 2), ("seq", 4)),
    "down": (("seq", 1), ("dp", 2), ("seq", 2), ("dp", 1), ("seq", 4)),
}


def stages_of(name):
    dp, seq = lax.axis_size("dp"), lax.axis_size("seq")
    places = []
    for axis, size in (("dp", dp), ("seq", seq)):
        bit = size // 2
        while bit:
            places.append((axis, bit))
            bit //= 2
    order = [stage for stage in ORDERS[name] if stage in places]
    order += [stage for stage in places if stage not in order]
    return places, order


def swap(array, axis, bit):
    size = lax.axis_size(axis)
    return lax.ppermute(array, axis, [(i, i ^ bit) for i in range(size)])


def gather_rows(array, name):
    places, order = stages_of(name)
    held = []
    rows, columns = array.shape
    for axis, bit in reversed(order):
        at = places.index((axis, bit))
        before = 2 ** sum(places.index(other) < at for other in held)
        view = array.reshape(before, -1, columns)
        other = swap(view, axis, bit)
        high = (lax.axis_index(axis) & bit) != 0
        array = jnp.stack(
            [jnp.where(high, other, view), jnp.where(high, view, other)], axis=1
        ).reshape(-1, columns)
        held.append((axis, bit))
    return array


def scatter_rows(array, name, kind=jnp.bfloat16):
    places, order = stages_of(name)
    left = list(places)
    columns = array.shape[-1]
    array = array.astype(kind)
    for axis, bit in order:
        at = left.index((axis, bit))
        view = array.reshape(2**at, 2, -1, columns)
        high = ((lax.axis_index(axis) & bit) != 0).astype(jnp.int32)
        mine = lax.dynamic_index_in_dim(view, high, 1, keepdims=False)
        theirs = lax.dynamic_index_in_dim(view, 1 - high, 1, keepdims=False)
        total = mine.astype(jnp.float32) + swap(theirs, axis, bit).astype(jnp.float32)
        left.remove((axis, bit))
        array = total.astype(kind) if left else total
    return array.reshape(-1, columns)


def pairs_per_device(seqs):
    return -(-seqs * HEADS // lax.axis_size("seq"))


def to_pairs(array):
    seqs, block, width = array.shape
    parts = width // D
    size, per = lax.axis_size("seq"), pairs_per_device(seqs)
    turned = array.transpose(0, 2, 1).reshape(seqs, parts, HEADS, HEAD_DIM, block)
    turned = turned.transpose(0, 2, 1, 3, 4).reshape(seqs * HEADS, parts * HEAD_DIM, block)
    turned = jnp.pad(turned, ((0, size * per - seqs * HEADS), (0, 0), (0, 0)))
    moved = lax.all_to_all(
        turned.reshape(size, per, parts * HEAD_DIM, block), "seq", 0, 0, tiled=False
    )
    return moved.transpose(1, 2, 0, 3).reshape(per, parts, HEAD_DIM, size * block)


def to_rows(array, seqs):
    per, parts, _, span = array.shape
    size = lax.axis_size("seq")
    block = span // size
    turned = array.reshape(per, parts * HEAD_DIM, size, block).transpose(2, 0, 1, 3)
    moved = lax.all_to_all(turned, "seq", 0, 0, tiled=False)
    moved = moved.reshape(size * per, parts, HEAD_DIM, block)[: seqs * HEADS]
    moved = moved.reshape(seqs, HEADS, parts, HEAD_DIM, block).transpose(0, 4, 2, 1, 3)
    return moved.reshape(seqs, block, parts * D)


def scores_for(query, key, live_keys):
    raw = jnp.einsum("pfq,pfk->pqk", query, key, preferred_element_type=jnp.float32)
    return jnp.where(live_keys[:, None, :], raw * (1.0 / math.sqrt(HEAD_DIM)), MASKED)


def attend(query, key, value, live_keys):
    scores = scores_for(query, key, live_keys)
    peak = jnp.max(scores, axis=-1)
    log_total = peak + jnp.log(jnp.sum(jnp.exp(scores - peak[..., None]), axis=-1))
    probs = jnp.exp(scores - log_total[..., None]).astype(jnp.bfloat16)
    mixed = jnp.einsum("pqk,pfk->pfq", probs, value, preferred_element_type=jnp.float32)
    return (log_total, mixed)


def attend_back(query, key, value, live_keys, log_total, mixed_full, mixed_grad):
    scale = 1.0 / math.sqrt(HEAD_DIM)
    delta = jnp.sum(mixed_grad.astype(jnp.float32) * mixed_full, axis=1)
    probs = jnp.exp(scores_for(query, key, live_keys) - log_total[..., None])
    grad_probs = jnp.einsum("pfq,pfk->pqk", mixed_grad, value, preferred_element_type=jnp.float32)
    grad_scores = (probs * (grad_probs - delta[..., None])).astype(jnp.bfloat16)
    probs = probs.astype(jnp.bfloat16)
    query_grad = (
        jnp.einsum("pqk,pfk->pfq", grad_scores, key, preferred_element_type=jnp.float32) * scale
    )
    key_grad = (
        jnp.einsum("pqk,pfq->pfk", grad_scores, query, preferred_element_type=jnp.float32) * scale
    )
    value_grad = jnp.einsum("pqk,pfq->pfk", probs, mixed_grad, preferred_element_type=jnp.float32)
    return jnp.stack([query_grad, key_grad, value_grad], axis=1).astype(jnp.bfloat16)


def forward_layer(state, weights, live_keys):
    w_in, w_out, w_hid, w_back, gain, bias, bias_h = weights
    gain = gain.astype(jnp.float32)
    bias = bias.astype(jnp.float32)
    bias_h = bias_h.astype(jnp.float32)
    lowered = state.astype(jnp.bfloat16)
    projected = jnp.dot(lowered, w_in, preferred_element_type=jnp.float32)
    query = (projected[..., :D] + bias[0]).astype(jnp.bfloat16)
    key = projected[..., D : 2 * D].astype(jnp.bfloat16)
    value = (projected[..., 2 * D :] + bias[1]).astype(jnp.bfloat16)
    pairs = to_pairs(jnp.concatenate((query, key, value), axis=-1))
    log_total, mixed_full = attend(pairs[:, 0], pairs[:, 1], pairs[:, 2], live_keys)
    mixed = to_rows(mixed_full.astype(jnp.bfloat16)[:, None], state.shape[0])
    first_sum = state + (jnp.dot(mixed, w_out, preferred_element_type=jnp.float32) + bias[2])
    normed = layer_norm(first_sum, gain[0], bias[4])
    normed_low = normed.astype(jnp.bfloat16)
    hidden = jnp.dot(normed_low, w_hid, preferred_element_type=jnp.float32) + bias_h
    activated = jax.nn.gelu(hidden, approximate=False).astype(jnp.bfloat16)
    second_sum = normed + (jnp.dot(activated, w_back, preferred_element_type=jnp.float32) + bias[3])
    result = layer_norm(second_sum, gain[1], bias[5])
    saved = (
        lowered,
        pairs,
        log_total,
        mixed_full,
        mixed,
        first_sum,
        normed_low,
        hidden,
        activated,
        second_sum,
    )
    return (result, saved)


def backward_layer(upstream, weights, saved, live_keys):
    w_in, w_out, w_hid, w_back, gain, bias, bias_h = weights
    gain = gain.astype(jnp.float32)
    bias = bias.astype(jnp.float32)
    (
        lowered,
        pairs,
        log_total,
        mixed_full,
        mixed,
        first_sum,
        normed_low,
        hidden,
        activated,
        second_sum,
    ) = saved
    grad_second, grad_gain_two, grad_shift_two = norm_back(second_sum, gain[1], bias[5], upstream)
    down_grad = grad_second.astype(jnp.bfloat16)
    grad_bias_down = jnp.sum(grad_second, axis=(0, 1))
    grad_down_w = jnp.einsum(
        "sqf,sqd->fd", activated, down_grad, preferred_element_type=jnp.float32
    )
    grad_activated = jnp.einsum(
        "sqd,fd->sqf", down_grad, w_back, preferred_element_type=jnp.float32
    )
    hidden_grad = gelu_back(hidden, grad_activated).astype(jnp.bfloat16)
    grad_bias_h = jnp.sum(hidden_grad.astype(jnp.float32), axis=(0, 1))
    grad_up_w = jnp.einsum(
        "sqd,sqf->df", normed_low, hidden_grad, preferred_element_type=jnp.float32
    )
    grad_normed = grad_second + jnp.einsum(
        "sqf,df->sqd", hidden_grad, w_hid, preferred_element_type=jnp.float32
    )
    grad_first, grad_gain_one, grad_shift_one = norm_back(first_sum, gain[0], bias[4], grad_normed)
    out_grad = grad_first.astype(jnp.bfloat16)
    grad_bias_out = jnp.sum(grad_first, axis=(0, 1))
    grad_out_w = jnp.einsum("sqd,sqe->de", mixed, out_grad, preferred_element_type=jnp.float32)
    mixed_grad = jnp.einsum(
        "sqe,de->sqd", out_grad, w_out, preferred_element_type=jnp.float32
    ).astype(jnp.bfloat16)
    pairs_grad = attend_back(
        pairs[:, 0],
        pairs[:, 1],
        pairs[:, 2],
        live_keys,
        log_total,
        mixed_full,
        to_pairs(mixed_grad)[:, 0],
    )
    projected_grad = to_rows(pairs_grad, mixed_grad.shape[0])
    grad_bias_query = jnp.sum(projected_grad[..., :D].astype(jnp.float32), axis=(0, 1))
    grad_bias_value = jnp.sum(projected_grad[..., 2 * D :].astype(jnp.float32), axis=(0, 1))
    grad_in_w = jnp.einsum(
        "sqd,sqe->de", lowered, projected_grad, preferred_element_type=jnp.float32
    )
    grad_state = grad_first + jnp.einsum(
        "sqe,de->sqd", projected_grad, w_in, preferred_element_type=jnp.float32
    )
    grad_gains_now = jnp.stack([grad_gain_one, grad_gain_two])
    grad_biases_now = jnp.stack(
        [
            grad_bias_query,
            grad_bias_value,
            grad_bias_out,
            grad_bias_down,
            grad_shift_one,
            grad_shift_two,
        ]
    )
    terms = (
        grad_in_w,
        grad_out_w,
        grad_up_w,
        grad_down_w,
        grad_gains_now,
        grad_biases_now,
        grad_bias_h,
    )
    return (grad_state, terms)


def per_device(
    hidden_in, lengths, w_attn_in, w_attn_out, w_up, w_down, gains, biases, bias_hidden, grad_out
):
    seqs, block, width = hidden_in.shape
    span = block * lax.axis_size("seq")
    first_row = lax.axis_index("seq") * block
    per = pairs_per_device(seqs)
    first_pair = lax.axis_index("seq") * per
    sequence_of = jnp.minimum((first_pair + jnp.arange(per, dtype=jnp.int32)) // HEADS, seqs - 1)
    pair_lengths = jnp.take(lengths, sequence_of)
    live_keys = jnp.arange(span, dtype=jnp.int32)[None, :] < pair_lengths[:, None]
    live_rows = (
        (first_row + jnp.arange(block, dtype=jnp.int32))[None, :] < lengths[:, None]
    ).astype(jnp.float32)
    state = hidden_in.astype(jnp.float32)
    devices = lax.axis_size("dp") * lax.axis_size("seq")
    thin = gains.shape[2]
    small = jnp.concatenate(
        [gains.reshape(LAYERS, -1), biases.reshape(LAYERS, -1), bias_hidden], axis=1
    ).reshape(1, -1)
    small = gather_rows(small, "in").reshape(devices, LAYERS, -1)
    split = 2 * thin
    stored = []
    for layer in range(LAYERS):
        weights = (
            gather_rows(w_attn_in[layer], "in"),
            gather_rows(w_attn_out[layer], "out"),
            gather_rows(w_up[layer], "up"),
            gather_rows(w_down[layer], "down"),
            small[:, layer, :split].reshape(devices, 2, thin).transpose(1, 0, 2).reshape(2, D),
            small[:, layer, split : 4 * split]
            .reshape(devices, 6, thin)
            .transpose(1, 0, 2)
            .reshape(6, D),
            small[:, layer, 4 * split :].reshape(-1),
        )
        state, saved = forward_layer(state, weights, live_keys)
        stored.append((weights, saved))
    upstream = grad_out.astype(jnp.float32) * live_rows[..., None]
    collected = []
    for layer in reversed(range(LAYERS)):
        weights, saved = stored[layer]
        upstream, terms = backward_layer(upstream, weights, saved, live_keys)
        thin_terms = jnp.concatenate(
            [
                terms[4].reshape(2, devices, thin).transpose(1, 0, 2).reshape(devices, -1),
                terms[5].reshape(6, devices, thin).transpose(1, 0, 2).reshape(devices, -1),
                terms[6].reshape(devices, -1),
            ],
            axis=1,
        )
        summed = scatter_rows(thin_terms, "out", jnp.float32)[0]
        collected.insert(
            0,
            (
                scatter_rows(terms[0], "in"),
                scatter_rows(terms[1], "out"),
                scatter_rows(terms[2], "up"),
                scatter_rows(terms[3], "down"),
                summed[:split].reshape(2, thin),
                summed[split : 4 * split].reshape(6, thin),
                summed[4 * split :],
            ),
        )
    stacked = tuple((jnp.stack([shares[member] for shares in collected]) for member in range(7)))
    return (state.astype(jnp.bfloat16), upstream.astype(jnp.bfloat16)) + stacked


def solution(mesh):
    placed = (
        P("dp", "seq", None),
        P("dp"),
        P(None, ("dp", "seq"), None),
        P(None, ("dp", "seq"), None),
        P(None, ("dp", "seq"), None),
        P(None, ("dp", "seq"), None),
        P(None, None, ("dp", "seq")),
        P(None, None, ("dp", "seq")),
        P(None, ("dp", "seq")),
        P("dp", "seq", None),
    )
    return jax.shard_map(
        per_device,
        mesh=mesh,
        in_specs=placed,
        out_specs=(
            P("dp", "seq", None),
            P("dp", "seq", None),
            P(None, ("dp", "seq"), None),
            P(None, ("dp", "seq"), None),
            P(None, ("dp", "seq"), None),
            P(None, ("dp", "seq"), None),
            P(None, None, ("dp", "seq")),
            P(None, None, ("dp", "seq")),
            P(None, ("dp", "seq")),
        ),
        check_vma=False,
    )
```

time: 2170 us -> 864 us (0.40)
  waiting for transfers between devices: 1400 us -> 335 us
  blocking collectives: 210 us -> 0 us
  starting transfers between devices: 1.15 us -> 140 us
  matrix products: 247 us -> 114 us
  local copies, waits for them, and re-layouts: 194 us -> 142 us
  other arithmetic: 85.9 us -> 116 us
    reduce_scatter x8 -> x0, waiting for transfers between devices: 756 us -> none  [the longest x2 281 us: per_device(): lax.psum_scatter(terms[3], ('dp', 'seq'), scatter_dimension=0, tiled=True)]
    unnamed x26 -> x0, waiting for transfers between devices: 372 us -> none
    ppermute x0 -> x95, waiting for transfers between devices: none -> 284 us  [swap(): return lax.ppermute(array, axis, [(i, i ^ bit) for i in range(size)])]
    all_gather x12 -> x0, waiting for transfers between devices: 269 us -> none  [the longest x2 124 us: per_device(): lax.all_gather(w_attn_in[layer], ('dp', 'seq'), axis=0, tiled=True)]
    all_gather x4 -> x0, blocking collectives: 171 us -> none  [the longest x2 87.2 us: per_device(): lax.all_gather(biases[layer], ('dp', 'seq'), axis=1, tiled=True)]
    ppermute x0 -> x95, starting transfers between devices: none -> 107 us  [swap(): return lax.ppermute(array, axis, [(i, i ^ bit) for i in range(size)])]
    dot_general x28 -> x12, matrix products: 150 us -> 49.1 us  [the longest x2 14.3 us: attend_back(): jnp.einsum('pfq,pfk->pqk', mixed_grad, value, preferred_element_type=jnp....]
    dynamic_slice x48 -> x2, local copies, waits for them, and re-layouts: 54.8 us -> 0.1 us  [scatter_rows(): mine = lax.dynamic_index_in_dim(view, high, 1, keepdims=False)]
  transfers between devices with their start and end apart: 23 -> 103, of which waited for: 16 -> 45; matrix products, arithmetic and copies ran while one was open for 16% -> 38% of each run, Pallas kernels for 0% -> 0%
where the time goes in v1:
time: 864 us; the launch traced here: 851 us
  waiting for transfers between devices  335 us (39%)
  local copies, waits for them, and re-layouts  142 us (16%)
  starting transfers between devices  140 us (16%)
  other arithmetic  116 us (13%)
  matrix products  114 us (13%)
    ppermute x95, waiting for transfers between devices, swap(): return lax.ppermute(array, axis, [(i, i ^ bit) for i in range(size)])  284 us
    ppermute x95, starting transfers between devices, swap(): return lax.ppermute(array, axis, [(i, i ^ bit) for i in range(size)])  107 us
    all_to_all x4, waiting for transfers between devices, to_pairs(): lax.all_to_all(turned.reshape(size, per, parts * HEAD_DIM, block), 'seq',...  36.3 us
    another operation x82, other arithmetic, gather_rows(): jnp.stack([jnp.where(high, other, view), jnp.where(high, view, other)], a...  31.7 us
    convert_element_type x32, other arithmetic, scatter_rows(): array = total.astype(kind) if left else total  30.8 us
    squeeze x48, local copies, waits for them, and re-layouts, scatter_rows(): theirs = lax.dynamic_index_in_dim(view, 1 - high, 1, keepdims=False)  28.8 us
    unnamed x250, local copies, waits for them, and re-layouts  21.5 us
  transfers between devices with their start and end apart: 103, of which 45 were waited for; matrix products, arithmetic and copies ran while one was open for 38% of the time, Pallas kernels for 0%

profile of v1, /device:TPU:0, one launch (start us, length us, event | category | flops | bytes accessed | tf_op | source)
XLA Modules:
  0.0 851.4 jit_solution(10182045564657004908)
XLA Ops:
  70.5 8.5 collective-permute-done.35
  92.1 10.6 %collective-permute-done.13 = bf16[2,96,768]{2,1,0:T(8,128)(2,1)S(1)} collective-permute-done((bf16[2,96,768]{2,1,0:T(8,128)(2,1)S(1)}, bf16[2,96,768]{2,1,0:T(8,128)(2,1)S(1)}, u32[]{:S(2)}, u32[]{:S(2)}) %collective-permute-start.13) | collective-permute-done | bytes 294944 | tf_op jit(solution)/shard_map/ppermute | solution.py:58
  105.3 6.9 collective-permute-done.2
  123.4 8.3 collective-permute-done.22
  145.8 16.9 %collective-permute-done.28 = bf16[1,192,2304]{2,1,0:T(8,128)(2,1)S(1)} collective-permute-done((bf16[1,192,2304]{2,1,0:T(8,128)(2,1)S(1)}, bf16[1,192,2304]{2,1,0:T(8,128)(2,1)S(1)}, u32[]{:S(2)}, u32[]{:S(2)}) %collective-permute-start.28) | collective-permute-done | bytes 884768 | tf_op jit(solution)/shard_map/ppermute | solution.py:58
  164.6 23.4 %collective-permute-done.43 = bf16[1,768,768]{2,1,0:T(8,128)(2,1)S(1)} collective-permute-done((bf16[1,768,768]{2,1,0:T(8,128)(2,1)S(1)}, bf16[1,768,768]{2,1,0:T(8,128)(2,1)S(1)}, u32[]{:S(2)}, u32[]{:S(2)}) %collective-permute-start.43) | collective-permute-done | bytes 1179680 | tf_op jit(solution)/shard_map/ppermute | solution.py:58
  192.2 20.3 %collective-permute-done.23 = bf16[1,768,768]{2,1,0:T(8,128)(2,1)S(1)} collective-permute-done((bf16[1,768,768]{2,1,0:T(8,128)(2,1)S(1)}, bf16[1,768,768]{2,1,0:T(8,128)(2,1)S(1)}, u32[]{:S(2)}, u32[]{:S(2)}) %collective-permute-start.23) | collective-permute-done | bytes 1179680 | tf_op jit(solution)/shard_map/ppermute | solution.py:58
  233.0 19.1 %all-to-all-done = bf16[8,3,192,128]{3,2,1,0:T(8,128)(2,1)} async-done(((bf16[8,3,192,128]{3,2,1,0:T(8,128)(2,1)}), bf16[8,3,192,128]{3,2,1,0:T(8,128)(2,1)}, u32[]{:S(2)}, u32[]{:S(2)}) %all-to-all-start) | async-done | bytes 1179680 | tf_op jit(solution)/shard_map/all_to_all | solution.py:106
  281.3 7.9 all-to-all-done.1
  296.1 8.0 multiply_convert_fusion.3
  330.8 17.2 %all-to-all-done.2 = bf16[8,3,192,128]{3,2,1,0:T(8,128)(2,1)} async-done(((bf16[8,3,192,128]{3,2,1,0:T(8,128)(2,1)}), bf16[8,3,192,128]{3,2,1,0:T(8,128)(2,1)}, u32[]{:S(2)}, u32[]{:S(2)}) %all-to-all-start.2) | async-done | bytes 1179680 | tf_op jit(solution)/shard_map/all_to_all | solution.py:106
  376.7 6.8 all-to-all-done.3
  390.7 7.6 multiply_convert_fusion.2
  440.1 6.5 fusion.38
  446.6 7.1 multiply_convert_fusion.1
  484.8 16.1 %collective-permute-done.64 = bf16[1,24,768]{2,1,0:T(8,128)(2,1)} collective-permute-done((bf16[1,24,768]{2,1,0:T(8,128)(2,1)}, bf16[1,24,768]{2,1,0:T(8,128)(2,1)}, u32[]{:S(2)}, u32[]{:S(2)}) %collective-permute-start.64) | collective-permute-done | bytes 36896 | tf_op jit(solution)/shard_map/ppermute | solution.py:58
  610.9 7.2 multiply_convert_fusion
  645.8 24.6 %collective-permute-done.58 = bf16[2,24,768]{2,1,0:T(8,128)(2,1)S(1)} collective-permute-done((bf16[2,24,768]{2,1,0:T(8,128)(2,1)S(1)}, bf16[2,24,768]{2,1,0:T(8,128)(2,1)S(1)}, u32[]{:S(2)}, u32[]{:S(2)}) %collective-permute-start.58) | collective-permute-done | bytes 73760 | tf_op jit(solution)/shard_map/ppermute | solution.py:58
  677.1 12.4 %collective-permute-done.72 = bf16[4,24,3072]{2,1,0:T(8,128)(2,1)S(1)} collective-permute-done((bf16[4,24,3072]{2,1,0:T(8,128)(2,1)S(1)}, bf16[4,24,3072]{2,1,0:T(8,128)(2,1)S(1)}, u32[]{:S(2)}, u32[]{:S(2)}) %collective-permute-start.72) | collective-permute-done | bytes 589856 | tf_op jit(solution)/shard_map/ppermute | solution.py:58
  726.6 19.2 %collective-permute-done.86 = f32[2,4,288]{2,1,0:T(4,128)S(1)} collective-permute-done((f32[2,4,288]{2,1,0:T(4,128)S(1)}, f32[2,4,288]{2,1,0:T(4,128)S(1)}, u32[]{:S(2)}, u32[]{:S(2)}) %collective-permute-start.86) | collective-permute-done | bytes 9248 | tf_op jit(solution)/shard_map/ppermute | solution.py:58
  777.6 12.4 %collective-permute-done.77 = bf16[4,96,768]{2,1,0:T(8,128)(2,1)S(1)} collective-permute-done((bf16[4,96,768]{2,1,0:T(8,128)(2,1)S(1)}, bf16[4,96,768]{2,1,0:T(8,128)(2,1)S(1)}, u32[]{:S(2)}, u32[]{:S(2)}) %collective-permute-start.77) | collective-permute-done | bytes 589856 | tf_op jit(solution)/shard_map/ppermute | solution.py:58
  790.6 9.8 %collective-permute-done.67 = bf16[4,24,3072]{2,1,0:T(8,128)(2,1)S(1)} collective-permute-done((bf16[4,24,3072]{2,1,0:T(8,128)(2,1)S(1)}, bf16[4,24,3072]{2,1,0:T(8,128)(2,1)S(1)}, u32[]{:S(2)}, u32[]{:S(2)}) %collective-permute-start.67) | collective-permute-done | bytes 589856 | tf_op jit(solution)/shard_map/ppermute | solution.py:58
  813.0 13.4 %collective-permute-done.46 = bf16[1,192,2304]{2,1,0:T(8,128)(2,1)S(1)} collective-permute-done((bf16[1,192,2304]{2,1,0:T(8,128)(2,1)S(1)}, bf16[1,192,2304]{2,1,0:T(8,128)(2,1)S(1)}, u32[]{:S(2)}, u32[]{:S(2)}) %collective-permute-start.46) | collective-permute-done | bytes 884768 | tf_op jit(solution)/shard_map/ppermute | solution.py:58
  827.9 9.1 %collective-permute-done.47 = bf16[1,96,2304]{2,1,0:T(8,128)(2,1)S(1)} collective-permute-done((bf16[1,96,2304]{2,1,0:T(8,128)(2,1)S(1)}, bf16[1,96,2304]{2,1,0:T(8,128)(2,1)S(1)}, u32[]{:S(2)}, u32[]{:S(2)}) %collective-permute-start.47) | collective-permute-done | bytes 442400 | tf_op jit(solution)/shard_map/ppermute | solution.py:58
  (867 shorter events, 548.2 us)
Async XLA Ops:
  1.6 56.7 %collective-permute-start.40 = (bf16[1,96,768]{2,1,0:T(8,128)(2,1)S(1)}, bf16[1,96,768]{2,1,0:T(8,128)(2,1)S(1)}, u32[]{:S(2)}, u32[]{:S(2)}) collective-permute-start(bf16[1,96,768]{2,1,0:T(8,128)(2,1)S(1)} %slice.228), channel_id=1, source_target_pairs={{0,4},{1,5},{2,6},{3,7},{4,0},{5,1},{6,2},{7,3},{8,12},{9,13},{10,... | collective-permute-start | bytes 442376 | tf_op jit(solution)/shard_map/ppermute | solution.py:58
  6.5 42.0 %collective-permute-start.30 = (bf16[1,24,768]{2,1,0:T(8,128)(2,1)S(1)}, bf16[1,24,768]{2,1,0:T(8,128)(2,1)S(1)}, u32[]{:S(2)}, u32[]{:S(2)}) collective-permute-start(bf16[1,24,768]{2,1,0:T(8,128)(2,1)S(1)} %slice.221), channel_id=1, source_target_pairs={{0,4},{1,5},{2,6},{3,7},{4,0},{5,1},{6,2},{7,3},{8,12},{9,13},{10,... | collective-permute-start | bytes 110600 | tf_op jit(solution)/shard_map/ppermute | solution.py:58
  7.4 49.6 %collective-permute-start = (bf16[1,24,2304]{2,1,0:T(8,128)(2,1)S(1)}, bf16[1,24,2304]{2,1,0:T(8,128)(2,1)S(1)}, u32[]{:S(2)}, u32[]{:S(2)}) collective-permute-start(bf16[1,24,2304]{2,1,0:T(8,128)(2,1)S(1)} %slice.190), channel_id=1, source_target_pairs={{0,4},{1,5},{2,6},{3,7},{4,0},{5,1},{6,2},{7,3},{8,12},{9,13},{10,... | collective-permute-start | bytes 331784 | tf_op jit(solution)/shard_map/ppermute | solution.py:58
  13.7 45.6 %collective-permute-start.15 = (bf16[1,24,3072]{2,1,0:T(8,128)(2,1)S(1)}, bf16[1,24,3072]{2,1,0:T(8,128)(2,1)S(1)}, u32[]{:S(2)}, u32[]{:S(2)}) collective-permute-start(bf16[1,24,3072]{2,1,0:T(8,128)(2,1)S(1)} %slice.205), channel_id=1, source_target_pairs={{0,4},{1,5},{2,6},{3,7},{4,0},{5,1},{6,2},{7,3},{8,12},{9,13},{10,... | collective-permute-start | bytes 442376 | tf_op jit(solution)/shard_map/ppermute | solution.py:58
  105.0 213.6 %collective-permute-start.34 = (bf16[16,24,768]{2,1,0:T(8,128)(2,1)}, bf16[16,24,768]{2,1,0:T(8,128)(2,1)}, u32[]{:S(2)}, u32[]{:S(2)}) collective-permute-start(bf16[16,24,768]{2,1,0:T(8,128)(2,1)} %bitcast.143), channel_id=1, source_target_pairs={{0,1},{1,0},{2,3},{3,2},{4,5},{5,4},{6,7},{7,6},{8,9},{9,8},{10,11... | collective-permute-start | bytes 1769480 | tf_op jit(solution)/shard_map/ppermute | solution.py:58
  132.4 55.5 %collective-permute-start.43 = (bf16[1,768,768]{2,1,0:T(8,128)(2,1)S(1)}, bf16[1,768,768]{2,1,0:T(8,128)(2,1)S(1)}, u32[]{:S(2)}, u32[]{:S(2)}) collective-permute-start(bf16[1,768,768]{2,1,0:T(8,128)(2,1)S(1)} %bitcast.855), channel_id=1, source_target_pairs={{0,16},{8,24},{16,0},{24,8},{1,17},{9,25},{17,1},{25,9},{2,18},{10... | collective-permute-start | bytes 3538952 | tf_op jit(solution)/shard_map/ppermute | solution.py:58
  140.5 49.3 %collective-permute-start.18 = (bf16[2,96,3072]{2,1,0:T(8,128)(2,1)S(1)}, bf16[2,96,3072]{2,1,0:T(8,128)(2,1)S(1)}, u32[]{:S(2)}, u32[]{:S(2)}) collective-permute-start(bf16[2,96,3072]{2,1,0:T(8,128)(2,1)S(1)} %bitcast.851), channel_id=1, source_target_pairs={{0,8},{8,0},{16,24},{24,16},{1,9},{9,1},{17,25},{25,17},{2,10},{10... | collective-permute-start | bytes 3538952 | tf_op jit(solution)/shard_map/ppermute | solution.py:58
  143.7 68.8 %collective-permute-start.23 = (bf16[1,768,768]{2,1,0:T(8,128)(2,1)S(1)}, bf16[1,768,768]{2,1,0:T(8,128)(2,1)S(1)}, u32[]{:S(2)}, u32[]{:S(2)}) collective-permute-start(bf16[1,768,768]{2,1,0:T(8,128)(2,1)S(1)} %bitcast.853), channel_id=1, source_target_pairs={{0,16},{8,24},{16,0},{24,8},{1,17},{9,25},{17,1},{25,9},{2,18},{10... | collective-permute-start | bytes 3538952 | tf_op jit(solution)/shard_map/ppermute | solution.py:58
  162.7 158.4 %collective-permute-start.38 = (bf16[2,96,3072]{2,1,0:T(8,128)(2,1)}, bf16[2,96,3072]{2,1,0:T(8,128)(2,1)}, u32[]{:S(2)}, u32[]{:S(2)}) collective-permute-start(bf16[2,96,3072]{2,1,0:T(8,128)(2,1)} %bitcast.158), channel_id=1, source_target_pairs={{0,8},{8,0},{16,24},{24,16},{1,9},{9,1},{17,25},{25,17},{2,10},{10... | collective-permute-start | bytes 3538952 | tf_op jit(solution)/shard_map/ppermute | solution.py:58
  212.6 112.6 %collective-permute-start.44 = (bf16[16,96,768]{2,1,0:T(8,128)(2,1)}, bf16[16,96,768]{2,1,0:T(8,128)(2,1)}, u32[]{:S(2)}, u32[]{:S(2)}) collective-permute-start(bf16[16,96,768]{2,1,0:T(8,128)(2,1)} %bitcast.177), channel_id=1, source_target_pairs={{0,1},{1,0},{2,3},{3,2},{4,5},{5,4},{6,7},{7,6},{8,9},{9,8},{10,11... | collective-permute-start | bytes 7077896 | tf_op jit(solution)/shard_map/ppermute | solution.py:58
  222.8 53.9 %collective-permute-start.24 = (bf16[16,96,768]{2,1,0:T(8,128)(2,1)S(1)}, bf16[16,96,768]{2,1,0:T(8,128)(2,1)}, u32[]{:S(2)}, u32[]{:S(2)}) collective-permute-start(bf16[16,96,768]{2,1,0:T(8,128)(2,1)S(1)} %bitcast.840), channel_id=1, source_target_pairs={{0,1},{1,0},{2,3},{3,2},{4,5},{5,4},{6,7},{7,6},{8,9},{9,8},{10,11... | collective-permute-start | bytes 7077896 | tf_op jit(solution)/shard_map/ppermute | solution.py:58
  324.7 46.2 %collective-permute-start.39 = (bf16[16,24,3072]{2,1,0:T(8,128)(2,1)}, bf16[16,24,3072]{2,1,0:T(8,128)(2,1)}, u32[]{:S(2)}, u32[]{:S(2)}) collective-permute-start(bf16[16,24,3072]{2,1,0:T(8,128)(2,1)} %bitcast.161), channel_id=1, source_target_pairs={{0,1},{1,0},{2,3},{3,2},{4,5},{5,4},{6,7},{7,6},{8,9},{9,8},{10,11... | collective-permute-start | bytes 7077896 | tf_op jit(solution)/shard_map/ppermute | solution.py:58
  430.4 72.1 %collective-permute-start.80 = (bf16[16,96,768]{2,1,0:T(8,128)(2,1)}, bf16[16,96,768]{2,1,0:T(8,128)(2,1)}, u32[]{:S(2)}, u32[]{:S(2)}) collective-permute-start(bf16[16,96,768]{2,1,0:T(8,128)(2,1)} %dynamic-slice_bitcast_fusion), channel_id=1, source_target_pairs={{0,1},{1,0},{2,3},{3,2},{4,5},{5,4},{6,7},{7,6},{8,9},{9,8},{10,11... | collective-permute-start | bytes 7077896 | tf_op jit(solution)/shard_map/ppermute | solution.py:58
  433.7 74.8 %collective-permute-start.70 = (bf16[16,24,3072]{2,1,0:T(8,128)(2,1)}, bf16[16,24,3072]{2,1,0:T(8,128)(2,1)}, u32[]{:S(2)}, u32[]{:S(2)}) collective-permute-start(bf16[16,24,3072]{2,1,0:T(8,128)(2,1)} %dynamic-slice_bitcast_fusion.2), channel_id=1, source_target_pairs={{0,1},{1,0},{2,3},{3,2},{4,5},{5,4},{6,7},{7,6},{8,9},{9,8},{10,11... | collective-permute-start | bytes 7077896 | tf_op jit(solution)/shard_map/ppermute | solution.py:58
  465.6 49.8 %all-to-all-start.5 = ((bf16[8,3,192,128]{3,2,1,0:T(8,128)(2,1)}), bf16[8,3,192,128]{3,2,1,0:T(8,128)(2,1)}, u32[]{:S(2)}, u32[]{:S(2)}) async-start(bf16[8,3,192,128]{3,2,1,0:T(8,128)(2,1)} %copy.439), calls=%async_computation.5 | async-start | bytes 2359296 | tf_op jit(solution)/shard_map/all_to_all | solution.py:117
  506.8 129.3 %collective-permute-start.81 = (bf16[1,768,768]{2,1,0:T(8,128)(2,1)}, bf16[1,768,768]{2,1,0:T(8,128)(2,1)}, u32[]{:S(2)}, u32[]{:S(2)}) collective-permute-start(bf16[1,768,768]{2,1,0:T(8,128)(2,1)} %dynamic-slice_bitcast_fusion.6), channel_id=1, source_target_pairs={{0,16},{8,24},{16,0},{24,8},{1,17},{9,25},{17,1},{25,9},{2,18},{10... | collective-permute-start | bytes 3538952 | tf_op jit(solution)/shard_map/ppermute | solution.py:58
  513.7 130.4 %collective-permute-start.71 = (bf16[2,96,3072]{2,1,0:T(8,128)(2,1)}, bf16[2,96,3072]{2,1,0:T(8,128)(2,1)}, u32[]{:S(2)}, u32[]{:S(2)}) collective-permute-start(bf16[2,96,3072]{2,1,0:T(8,128)(2,1)} %dynamic-slice_bitcast_fusion.8), channel_id=1, source_target_pairs={{0,8},{8,0},{16,24},{24,16},{1,9},{9,1},{17,25},{25,17},{2,10},{10... | collective-permute-start | bytes 3538952 | tf_op jit(solution)/shard_map/ppermute | solution.py:58
  592.8 113.8 %collective-permute-start.75 = (bf16[16,96,768]{2,1,0:T(8,128)(2,1)}, bf16[16,96,768]{2,1,0:T(8,128)(2,1)}, u32[]{:S(2)}, u32[]{:S(2)}) collective-permute-start(bf16[16,96,768]{2,1,0:T(8,128)(2,1)} %dynamic-slice_bitcast_fusion.1), channel_id=1, source_target_pairs={{0,1},{1,0},{2,3},{3,2},{4,5},{5,4},{6,7},{7,6},{8,9},{9,8},{10,11... | collective-permute-start | bytes 7077896 | tf_op jit(solution)/shard_map/ppermute | solution.py:58
  599.2 112.1 %collective-permute-start.65 = (bf16[16,24,3072]{2,1,0:T(8,128)(2,1)}, bf16[16,24,3072]{2,1,0:T(8,128)(2,1)}, u32[]{:S(2)}, u32[]{:S(2)}) collective-permute-start(bf16[16,24,3072]{2,1,0:T(8,128)(2,1)} %dynamic-slice_bitcast_fusion.3), channel_id=1, source_target_pairs={{0,1},{1,0},{2,3},{3,2},{4,5},{5,4},{6,7},{7,6},{8,9},{9,8},{10,11... | collective-permute-start | bytes 7077896 | tf_op jit(solution)/shard_map/ppermute | solution.py:58
  629.8 86.9 %all-to-all-start.7 = ((bf16[8,3,192,128]{3,2,1,0:T(8,128)(2,1)}), bf16[8,3,192,128]{3,2,1,0:T(8,128)(2,1)}, u32[]{:S(2)}, u32[]{:S(2)}) async-start(bf16[8,3,192,128]{3,2,1,0:T(8,128)(2,1)} %copy.449), calls=%async_computation.7 | async-start | bytes 2359296 | tf_op jit(solution)/shard_map/all_to_all | solution.py:117
  634.3 64.4 %collective-permute-start.50 = (bf16[16,24,2304]{2,1,0:T(8,128)(2,1)}, bf16[16,24,2304]{2,1,0:T(8,128)(2,1)S(1)}, u32[]{:S(2)}, u32[]{:S(2)}) collective-permute-start(bf16[16,24,2304]{2,1,0:T(8,128)(2,1)} %dynamic-slice_bitcast_fusion.4), channel_id=1, source_target_pairs={{0,1},{1,0},{2,3},{3,2},{4,5},{5,4},{6,7},{7,6},{8,9},{9,8},{10,11... | collective-permute-start | bytes 5308424 | tf_op jit(solution)/shard_map/ppermute | solution.py:58
  710.7 61.1 %collective-permute-start.76 = (bf16[1,768,768]{2,1,0:T(8,128)(2,1)}, bf16[1,768,768]{2,1,0:T(8,128)(2,1)}, u32[]{:S(2)}, u32[]{:S(2)}) collective-permute-start(bf16[1,768,768]{2,1,0:T(8,128)(2,1)} %dynamic-slice_bitcast_fusion.7), channel_id=1, source_target_pairs={{0,16},{8,24},{16,0},{24,8},{1,17},{9,25},{17,1},{25,9},{2,18},{10... | collective-permute-start | bytes 3538952 | tf_op jit(solution)/shard_map/ppermute | solution.py:58
  716.4 58.5 %collective-permute-start.66 = (bf16[2,96,3072]{2,1,0:T(8,128)(2,1)}, bf16[2,96,3072]{2,1,0:T(8,128)(2,1)}, u32[]{:S(2)}, u32[]{:S(2)}) collective-permute-start(bf16[2,96,3072]{2,1,0:T(8,128)(2,1)} %dynamic-slice_bitcast_fusion.9), channel_id=1, source_target_pairs={{0,8},{8,0},{16,24},{24,16},{1,9},{9,1},{17,25},{25,17},{2,10},{10... | collective-permute-start | bytes 3538952 | tf_op jit(solution)/shard_map/ppermute | solution.py:58
  758.2 45.5 %collective-permute-start.45 = (bf16[16,24,2304]{2,1,0:T(8,128)(2,1)}, bf16[16,24,2304]{2,1,0:T(8,128)(2,1)}, u32[]{:S(2)}, u32[]{:S(2)}) collective-permute-start(bf16[16,24,2304]{2,1,0:T(8,128)(2,1)} %dynamic-slice_bitcast_fusion.5), channel_id=1, source_target_pairs={{0,1},{1,0},{2,3},{3,2},{4,5},{5,4},{6,7},{7,6},{8,9},{9,8},{10,11... | collective-permute-start | bytes 5308424 | tf_op jit(solution)/shard_map/ppermute | solution.py:58
  (196 other events, 2134.2 us)

commit v2 on v1

--- a/solution.py
+++ b/solution.py
@@ -90,6 +90,10 @@
         left.remove((axis, bit))
         array = total.astype(kind) if left else total
     return array.reshape(-1, columns)
+
+
+def after(array, done):
+    return lax.optimization_barrier((array, done))
 
 
 def pairs_per_device(seqs):
@@ -186,7 +190,7 @@
     return (result, saved)
 
 
-def backward_layer(upstream, weights, saved, live_keys):
+def backward_layer(upstream, weights, saved, live_keys, finished):
     w_in, w_out, w_hid, w_back, gain, bias, bias_h = weights
     gain = gain.astype(jnp.float32)
     bias = bias.astype(jnp.float32)
@@ -226,6 +230,9 @@
     mixed_grad = jnp.einsum(
         "sqe,de->sqd", out_grad, w_out, preferred_element_type=jnp.float32
     ).astype(jnp.bfloat16)
+    mixed_pairs = to_pairs(mixed_grad)[:, 0]
+    if finished is not None:
+        mixed_pairs, finished = after(mixed_pairs, finished)
     pairs_grad = attend_back(
         pairs[:, 0],
         pairs[:, 1],
@@ -233,7 +240,7 @@
         live_keys,
         log_total,
         mixed_full,
-        to_pairs(mixed_grad)[:, 0],
+        mixed_pairs,
     )
     projected_grad = to_rows(pairs_grad, mixed_grad.shape[0])
     grad_bias_query = jnp.sum(projected_grad[..., :D].astype(jnp.float32), axis=(0, 1))
@@ -264,7 +271,7 @@
         grad_biases_now,
         grad_bias_h,
     )
-    return (grad_state, terms)
+    return (grad_state, terms, finished)
 
 
 def per_device(
@@ -290,12 +297,20 @@
     small = gather_rows(small, "in").reshape(devices, LAYERS, -1)
     split = 2 * thin
     stored = []
+    ready = None
     for layer in range(LAYERS):
+        shard_in = w_attn_in[layer]
+        if ready is not None:
+            shard_in, _ = after(shard_in, ready)
+        full_in = gather_rows(shard_in, "in")
+        (shard_out, shard_up, shard_down), full_in = after(
+            (w_attn_out[layer], w_up[layer], w_down[layer]), full_in
+        )
         weights = (
-            gather_rows(w_attn_in[layer], "in"),
-            gather_rows(w_attn_out[layer], "out"),
-            gather_rows(w_up[layer], "up"),
-            gather_rows(w_down[layer], "down"),
+            full_in,
+            gather_rows(shard_out, "out"),
+            gather_rows(shard_up, "up"),
+            gather_rows(shard_down, "down"),
             small[:, layer, :split].reshape(devices, 2, thin).transpose(1, 0, 2).reshape(2, D),
             small[:, layer, split : 4 * split]
             .reshape(devices, 6, thin)
@@ -304,12 +319,16 @@
             small[:, layer, 4 * split :].reshape(-1),
         )
         state, saved = forward_layer(state, weights, live_keys)
+        ready = saved[2]
         stored.append((weights, saved))
     upstream = grad_out.astype(jnp.float32) * live_rows[..., None]
     collected = []
     for layer in reversed(range(LAYERS)):
         weights, saved = stored[layer]
-        upstream, terms = backward_layer(upstream, weights, saved, live_keys)
+        finished = collected[0] if collected else None
+        upstream, terms, finished = backward_layer(upstream, weights, saved, live_keys, finished)
+        if collected:
+            collected[0] = finished
         thin_terms = jnp.concatenate(
             [
                 terms[4].reshape(2, devices, thin).transpose(1, 0, 2).reshape(devices, -1),

time: 864 us -> 865 us (level)
  local copies, waits for them, and re-layouts: 142 us -> 173 us
  waiting for transfers between devices: 335 us -> 315 us
  matrix products: 114 us -> 97.7 us
    all_to_all x4, waiting for transfers between devices: 36.3 us -> 16.9 us  [to_pairs(): lax.all_to_all(turned.reshape(size, per, parts * HEAD_DIM, block), 'seq',...]
    all_to_all x4, waiting for transfers between devices: 14.7 us -> 2.21 us  [to_rows(): moved = lax.all_to_all(turned, 'seq', 0, 0, tiled=False)]
    ppermute x95, waiting for transfers between devices: 284 us -> 296 us  [swap(): return lax.ppermute(array, axis, [(i, i ^ bit) for i in range(size)])]
    another operation x82 -> x79, other arithmetic: 31.7 us -> 38 us  [gather_rows(): jnp.stack([jnp.where(high, other, view), jnp.where(high, view, other)], a...]
    unnamed x250 -> x302, local copies, waits for them, and re-layouts: 21.5 us -> 21.4 us
  transfers between devices with their start and end apart: 103 -> 103, of which waited for: 45 -> 52; matrix products, arithmetic and copies ran while one was open for 38% -> 40% of each run, Pallas kernels for 0% -> 0%
where the time goes in v2:
time: 865 us; the launch traced here: 855 us
  waiting for transfers between devices  315 us (36%)
  local copies, waits for them, and re-layouts  173 us (20%)
  starting transfers between devices  143 us (17%)
  other arithmetic  122 us (14%)
  matrix products  97.7 us (11%)
    ppermute x95, waiting for transfers between devices, swap(): return lax.ppermute(array, axis, [(i, i ^ bit) for i in range(size)])  296 us
    ppermute x95, starting transfers between devices, swap(): return lax.ppermute(array, axis, [(i, i ^ bit) for i in range(size)])  111 us
    another operation x79, other arithmetic, gather_rows(): jnp.stack([jnp.where(high, other, view), jnp.where(high, view, other)], a...  38 us
    convert_element_type x32, other arithmetic, scatter_rows(): array = total.astype(kind) if left else total  27.1 us
    squeeze x48, local copies, waits for them, and re-layouts, scatter_rows(): theirs = lax.dynamic_index_in_dim(view, 1 - high, 1, keepdims=False)  25.9 us
    unnamed x302, local copies, waits for them, and re-layouts  21.4 us
  transfers between devices with their start and end apart: 103, of which 52 were waited for; matrix products, arithmetic and copies ran while one was open for 40% of the time, Pallas kernels for 0%

profile of v2, /device:TPU:0, one launch (start us, length us, event | category | flops | bytes accessed | tf_op | source)
XLA Modules:
  0.0 855.0 jit_solution(1005088363769602334)
XLA Ops:
  47.0 6.8 collective-permute-done.2
  55.8 5.8 collective-permute-done.27
  63.4 13.2 %collective-permute-done.3 = bf16[1,192,2304]{2,1,0:T(8,128)(2,1)S(1)} collective-permute-done((bf16[1,192,2304]{2,1,0:T(8,128)(2,1)S(1)}, bf16[1,192,2304]{2,1,0:T(8,128)(2,1)S(1)}, u32[]{:S(2)}, u32[]{:S(2)}) %collective-permute-start.3) | collective-permute-done | bytes 884768 | tf_op jit(solution)/shard_map/ppermute | solution.py:58
  138.9 15.7 %collective-permute-done.11 = bf16[2,24,768]{2,1,0:T(8,128)(2,1)S(1)} collective-permute-done((bf16[2,24,768]{2,1,0:T(8,128)(2,1)S(1)}, bf16[2,24,768]{2,1,0:T(8,128)(2,1)S(1)}, u32[]{:S(2)}, u32[]{:S(2)}) %collective-permute-start.11) | collective-permute-done | bytes 73760 | tf_op jit(solution)/shard_map/ppermute | solution.py:58
  162.1 10.8 %collective-permute-done.15 = bf16[1,24,3072]{2,1,0:T(8,128)(2,1)S(1)} collective-permute-done((bf16[1,24,3072]{2,1,0:T(8,128)(2,1)S(1)}, bf16[1,24,3072]{2,1,0:T(8,128)(2,1)S(1)}, u32[]{:S(2)}, u32[]{:S(2)}) %collective-permute-start.15) | collective-permute-done | bytes 147488 | tf_op jit(solution)/shard_map/ppermute | solution.py:58
  185.8 6.7 collective-permute-done.32
  204.8 7.3 collective-permute-done.22
  212.1 25.3 %collective-permute-done.42 = bf16[4,96,768]{2,1,0:T(8,128)(2,1)S(1)} collective-permute-done((bf16[4,96,768]{2,1,0:T(8,128)(2,1)S(1)}, bf16[4,96,768]{2,1,0:T(8,128)(2,1)S(1)}, u32[]{:S(2)}, u32[]{:S(2)}) %collective-permute-start.42) | collective-permute-done | bytes 589856 | tf_op jit(solution)/shard_map/ppermute | solution.py:58
  241.1 5.6 collective-permute-done.37
  271.6 14.0 %collective-permute-done.23 = bf16[1,768,768]{2,1,0:T(8,128)(2,1)} collective-permute-done((bf16[1,768,768]{2,1,0:T(8,128)(2,1)S(1)}, bf16[1,768,768]{2,1,0:T(8,128)(2,1)}, u32[]{:S(2)}, u32[]{:S(2)}) %collective-permute-start.23) | collective-permute-done | bytes 1179680 | tf_op jit(solution)/shard_map/ppermute | solution.py:58
  292.6 5.8 collective-permute-done.38
  313.6 8.0 multiply_convert_fusion.3
  351.8 13.6 %all-to-all-done.2 = bf16[8,3,192,128]{3,2,1,0:T(8,128)(2,1)} async-done(((bf16[8,3,192,128]{3,2,1,0:T(8,128)(2,1)}), bf16[8,3,192,128]{3,2,1,0:T(8,128)(2,1)}, u32[]{:S(2)}, u32[]{:S(2)}) %all-to-all-start.2) | async-done | bytes 1179680 | tf_op jit(solution)/shard_map/all_to_all | solution.py:110
  408.3 7.4 multiply_convert_fusion.2
  458.0 6.5 fusion.53
  464.5 7.1 multiply_convert_fusion.1
  502.7 16.1 %collective-permute-done.54 = bf16[1,24,768]{2,1,0:T(8,128)(2,1)} collective-permute-done((bf16[1,24,768]{2,1,0:T(8,128)(2,1)}, bf16[1,24,768]{2,1,0:T(8,128)(2,1)}, u32[]{:S(2)}, u32[]{:S(2)}) %collective-permute-start.54) | collective-permute-done | bytes 36896 | tf_op jit(solution)/shard_map/ppermute | solution.py:58
  620.4 12.8 %collective-permute-done.78 = bf16[2,24,768]{2,1,0:T(8,128)(2,1)S(1)} collective-permute-done((bf16[2,24,768]{2,1,0:T(8,128)(2,1)S(1)}, bf16[2,24,768]{2,1,0:T(8,128)(2,1)S(1)}, u32[]{:S(2)}, u32[]{:S(2)}) %collective-permute-start.78) | collective-permute-done | bytes 73760 | tf_op jit(solution)/shard_map/ppermute | solution.py:58
  641.4 9.9 %collective-permute-done.57 = bf16[4,24,3072]{2,1,0:T(8,128)(2,1)S(1)} collective-permute-done((bf16[4,24,3072]{2,1,0:T(8,128)(2,1)S(1)}, bf16[4,24,3072]{2,1,0:T(8,128)(2,1)S(1)}, u32[]{:S(2)}, u32[]{:S(2)}) %collective-permute-start.57) | collective-permute-done | bytes 589856 | tf_op jit(solution)/shard_map/ppermute | solution.py:58
  667.9 12.2 %collective-permute-done.46 = bf16[1,192,2304]{2,1,0:T(8,128)(2,1)S(1)} collective-permute-done((bf16[1,192,2304]{2,1,0:T(8,128)(2,1)S(1)}, bf16[1,192,2304]{2,1,0:T(8,128)(2,1)S(1)}, u32[]{:S(2)}, u32[]{:S(2)}) %collective-permute-start.46) | collective-permute-done | bytes 884768 | tf_op jit(solution)/shard_map/ppermute | solution.py:58
  734.5 26.9 %collective-permute-done.87 = bf16[4,96,768]{2,1,0:T(8,128)(2,1)S(1)} collective-permute-done((bf16[4,96,768]{2,1,0:T(8,128)(2,1)S(1)}, bf16[4,96,768]{2,1,0:T(8,128)(2,1)S(1)}, u32[]{:S(2)}, u32[]{:S(2)}) %collective-permute-start.87) | collective-permute-done | bytes 589856 | tf_op jit(solution)/shard_map/ppermute | solution.py:58
  816.5 13.5 %collective-permute-done.71 = bf16[1,192,2304]{2,1,0:T(8,128)(2,1)S(1)} collective-permute-done((bf16[1,192,2304]{2,1,0:T(8,128)(2,1)S(1)}, bf16[1,192,2304]{2,1,0:T(8,128)(2,1)S(1)}, u32[]{:S(2)}, u32[]{:S(2)}) %collective-permute-start.71) | collective-permute-done | bytes 884768 | tf_op jit(solution)/shard_map/ppermute | solution.py:58
  832.3 7.1 collective-permute-done.72
  847.5 6.2 collective-permute-done.74
  (917 shorter events, 586.4 us)
Async XLA Ops:
  61.7 54.7 %collective-permute-start.28 = (bf16[1,192,2304]{2,1,0:T(8,128)(2,1)S(1)}, bf16[1,192,2304]{2,1,0:T(8,128)(2,1)S(1)}, u32[]{:S(2)}, u32[]{:S(2)}) collective-permute-start(bf16[1,192,2304]{2,1,0:T(8,128)(2,1)S(1)} %bitcast.959), channel_id=1, source_target_pairs={{0,16},{8,24},{16,0},{24,8},{1,17},{9,25},{17,1},{25,9},{2,18},{10... | collective-permute-start | bytes 2654216 | tf_op jit(solution)/shard_map/ppermute | solution.py:58
  120.0 41.1 %collective-permute-start.20 = (bf16[1,96,768]{2,1,0:T(8,128)(2,1)S(1)}, bf16[1,96,768]{2,1,0:T(8,128)(2,1)}, u32[]{:S(2)}, u32[]{:S(2)}) collective-permute-start(bf16[1,96,768]{2,1,0:T(8,128)(2,1)S(1)} %bitcast.1019), channel_id=1, source_target_pairs={{0,4},{1,5},{2,6},{3,7},{4,0},{5,1},{6,2},{7,3},{8,12},{9,13},{10,... | collective-permute-start | bytes 442376 | tf_op jit(solution)/shard_map/ppermute | solution.py:58
  125.6 125.9 %all-to-all-start = ((bf16[8,3,192,128]{3,2,1,0:T(8,128)(2,1)}), bf16[8,3,192,128]{3,2,1,0:T(8,128)(2,1)S(1)}, u32[]{:S(2)}, u32[]{:S(2)}) async-start(bf16[8,3,192,128]{3,2,1,0:T(8,128)(2,1)} %bitcast.928), calls=%async_computation | async-start | bytes 2359296 | tf_op jit(solution)/shard_map/all_to_all | solution.py:110
  129.6 43.2 %collective-permute-start.15 = (bf16[1,24,3072]{2,1,0:T(8,128)(2,1)S(1)}, bf16[1,24,3072]{2,1,0:T(8,128)(2,1)S(1)}, u32[]{:S(2)}, u32[]{:S(2)}) collective-permute-start(bf16[1,24,3072]{2,1,0:T(8,128)(2,1)S(1)} %bitcast.1018), channel_id=1, source_target_pairs={{0,4},{1,5},{2,6},{3,7},{4,0},{5,1},{6,2},{7,3},{8,12},{9,13},{10,... | collective-permute-start | bytes 442376 | tf_op jit(solution)/shard_map/ppermute | solution.py:58
  138.3 44.5 %collective-permute-start.40 = (bf16[1,96,768]{2,1,0:T(8,128)(2,1)S(1)}, bf16[1,96,768]{2,1,0:T(8,128)(2,1)S(1)}, u32[]{:S(2)}, u32[]{:S(2)}) collective-permute-start(bf16[1,96,768]{2,1,0:T(8,128)(2,1)S(1)} %bitcast.1017), channel_id=1, source_target_pairs={{0,4},{1,5},{2,6},{3,7},{4,0},{5,1},{6,2},{7,3},{8,12},{9,13},{10,... | collective-permute-start | bytes 442376 | tf_op jit(solution)/shard_map/ppermute | solution.py:58
  196.0 43.5 %collective-permute-start.17 = (bf16[4,24,3072]{2,1,0:T(8,128)(2,1)S(1)}, bf16[4,24,3072]{2,1,0:T(8,128)(2,1)S(1)}, u32[]{:S(2)}, u32[]{:S(2)}) collective-permute-start(bf16[4,24,3072]{2,1,0:T(8,128)(2,1)S(1)} %bitcast.961), channel_id=1, source_target_pairs={{0,2},{1,3},{2,0},{3,1},{4,6},{5,7},{6,4},{7,5},{8,10},{9,11},{10,... | collective-permute-start | bytes 1769480 | tf_op jit(solution)/shard_map/ppermute | solution.py:58
  199.8 46.8 %collective-permute-start.37 = (bf16[4,24,3072]{2,1,0:T(8,128)(2,1)S(1)}, bf16[4,24,3072]{2,1,0:T(8,128)(2,1)S(1)}, u32[]{:S(2)}, u32[]{:S(2)}) collective-permute-start(bf16[4,24,3072]{2,1,0:T(8,128)(2,1)S(1)} %bitcast.965), channel_id=1, source_target_pairs={{0,2},{1,3},{2,0},{3,1},{4,6},{5,7},{6,4},{7,5},{8,10},{9,11},{10,... | collective-permute-start | bytes 1769480 | tf_op jit(solution)/shard_map/ppermute | solution.py:58
  204.7 135.8 %collective-permute-start.34 = (bf16[16,24,768]{2,1,0:T(8,128)(2,1)}, bf16[16,24,768]{2,1,0:T(8,128)(2,1)}, u32[]{:S(2)}, u32[]{:S(2)}) collective-permute-start(bf16[16,24,768]{2,1,0:T(8,128)(2,1)} %bitcast.156), channel_id=1, source_target_pairs={{0,1},{1,0},{2,3},{3,2},{4,5},{5,4},{6,7},{7,6},{8,9},{9,8},{10,11... | collective-permute-start | bytes 1769480 | tf_op jit(solution)/shard_map/ppermute | solution.py:58
  238.8 104.3 %collective-permute-start.43 = (bf16[1,768,768]{2,1,0:T(8,128)(2,1)}, bf16[1,768,768]{2,1,0:T(8,128)(2,1)}, u32[]{:S(2)}, u32[]{:S(2)}) collective-permute-start(bf16[1,768,768]{2,1,0:T(8,128)(2,1)} %bitcast.189), channel_id=1, source_target_pairs={{0,16},{8,24},{16,0},{24,8},{1,17},{9,25},{17,1},{25,9},{2,18},{10... | collective-permute-start | bytes 3538952 | tf_op jit(solution)/shard_map/ppermute | solution.py:58
  239.5 46.1 %collective-permute-start.23 = (bf16[1,768,768]{2,1,0:T(8,128)(2,1)S(1)}, bf16[1,768,768]{2,1,0:T(8,128)(2,1)}, u32[]{:S(2)}, u32[]{:S(2)}) collective-permute-start(bf16[1,768,768]{2,1,0:T(8,128)(2,1)S(1)} %bitcast.909), channel_id=1, source_target_pairs={{0,16},{8,24},{16,0},{24,8},{1,17},{9,25},{17,1},{25,9},{2,18},{10... | collective-permute-start | bytes 3538952 | tf_op jit(solution)/shard_map/ppermute | solution.py:58
  248.0 40.6 %collective-permute-start.18 = (bf16[2,96,3072]{2,1,0:T(8,128)(2,1)}, bf16[2,96,3072]{2,1,0:T(8,128)(2,1)}, u32[]{:S(2)}, u32[]{:S(2)}) collective-permute-start(bf16[2,96,3072]{2,1,0:T(8,128)(2,1)} %bitcast.79), channel_id=1, source_target_pairs={{0,8},{8,0},{16,24},{24,16},{1,9},{9,1},{17,25},{25,17},{2,10},{10... | collective-permute-start | bytes 3538952 | tf_op jit(solution)/shard_map/ppermute | solution.py:58
  249.8 48.6 %collective-permute-start.38 = (bf16[2,96,3072]{2,1,0:T(8,128)(2,1)}, bf16[2,96,3072]{2,1,0:T(8,128)(2,1)}, u32[]{:S(2)}, u32[]{:S(2)}) collective-permute-start(bf16[2,96,3072]{2,1,0:T(8,128)(2,1)} %bitcast.172), channel_id=1, source_target_pairs={{0,8},{8,0},{16,24},{24,16},{1,9},{9,1},{17,25},{25,17},{2,10},{10... | collective-permute-start | bytes 3538952 | tf_op jit(solution)/shard_map/ppermute | solution.py:58
  301.9 45.0 %collective-permute-start.39 = (bf16[16,24,3072]{2,1,0:T(8,128)(2,1)}, bf16[16,24,3072]{2,1,0:T(8,128)(2,1)}, u32[]{:S(2)}, u32[]{:S(2)}) collective-permute-start(bf16[16,24,3072]{2,1,0:T(8,128)(2,1)} %bitcast.175), channel_id=1, source_target_pairs={{0,1},{1,0},{2,3},{3,2},{4,5},{5,4},{6,7},{7,6},{8,9},{9,8},{10,11... | collective-permute-start | bytes 7077896 | tf_op jit(solution)/shard_map/ppermute | solution.py:58
  346.5 42.1 %collective-permute-start.44 = (bf16[16,96,768]{2,1,0:T(8,128)(2,1)}, bf16[16,96,768]{2,1,0:T(8,128)(2,1)}, u32[]{:S(2)}, u32[]{:S(2)}) collective-permute-start(bf16[16,96,768]{2,1,0:T(8,128)(2,1)} %bitcast.192), channel_id=1, source_target_pairs={{0,1},{1,0},{2,3},{3,2},{4,5},{5,4},{6,7},{7,6},{8,9},{9,8},{10,11... | collective-permute-start | bytes 7077896 | tf_op jit(solution)/shard_map/ppermute | solution.py:58
  448.1 72.3 %collective-permute-start.60 = (bf16[16,96,768]{2,1,0:T(8,128)(2,1)}, bf16[16,96,768]{2,1,0:T(8,128)(2,1)}, u32[]{:S(2)}, u32[]{:S(2)}) collective-permute-start(bf16[16,96,768]{2,1,0:T(8,128)(2,1)} %dynamic-slice_bitcast_fusion.2), channel_id=1, source_target_pairs={{0,1},{1,0},{2,3},{3,2},{4,5},{5,4},{6,7},{7,6},{8,9},{9,8},{10,11... | collective-permute-start | bytes 7077896 | tf_op jit(solution)/shard_map/ppermute | solution.py:58
  451.5 73.8 %collective-permute-start.55 = (bf16[16,24,3072]{2,1,0:T(8,128)(2,1)}, bf16[16,24,3072]{2,1,0:T(8,128)(2,1)}, u32[]{:S(2)}, u32[]{:S(2)}) collective-permute-start(bf16[16,24,3072]{2,1,0:T(8,128)(2,1)} %dynamic-slice_bitcast_fusion.3), channel_id=1, source_target_pairs={{0,1},{1,0},{2,3},{3,2},{4,5},{5,4},{6,7},{7,6},{8,9},{9,8},{10,11... | collective-permute-start | bytes 7077896 | tf_op jit(solution)/shard_map/ppermute | solution.py:58
  483.6 48.4 %all-to-all-start.5 = ((bf16[8,3,192,128]{3,2,1,0:T(8,128)(2,1)}), bf16[8,3,192,128]{3,2,1,0:T(8,128)(2,1)}, u32[]{:S(2)}, u32[]{:S(2)}) async-start(bf16[8,3,192,128]{3,2,1,0:T(8,128)(2,1)} %copy.435), calls=%async_computation.5 | async-start | bytes 2359296 | tf_op jit(solution)/shard_map/all_to_all | solution.py:121
  524.7 85.5 %collective-permute-start.61 = (bf16[1,768,768]{2,1,0:T(8,128)(2,1)}, bf16[1,768,768]{2,1,0:T(8,128)(2,1)}, u32[]{:S(2)}, u32[]{:S(2)}) collective-permute-start(bf16[1,768,768]{2,1,0:T(8,128)(2,1)} %dynamic-slice_bitcast_fusion.8), channel_id=1, source_target_pairs={{0,16},{8,24},{16,0},{24,8},{1,17},{9,25},{17,1},{25,9},{2,18},{10... | collective-permute-start | bytes 3538952 | tf_op jit(solution)/shard_map/ppermute | solution.py:58
  530.5 88.0 %collective-permute-start.56 = (bf16[2,96,3072]{2,1,0:T(8,128)(2,1)}, bf16[2,96,3072]{2,1,0:T(8,128)(2,1)}, u32[]{:S(2)}, u32[]{:S(2)}) collective-permute-start(bf16[2,96,3072]{2,1,0:T(8,128)(2,1)} %dynamic-slice_bitcast_fusion.9), channel_id=1, source_target_pairs={{0,8},{8,0},{16,24},{24,16},{1,9},{9,1},{17,25},{25,17},{2,10},{10... | collective-permute-start | bytes 3538952 | tf_op jit(solution)/shard_map/ppermute | solution.py:58
  586.4 74.6 %collective-permute-start.45 = (bf16[16,24,2304]{2,1,0:T(8,128)(2,1)}, bf16[16,24,2304]{2,1,0:T(8,128)(2,1)}, u32[]{:S(2)}, u32[]{:S(2)}) collective-permute-start(bf16[16,24,2304]{2,1,0:T(8,128)(2,1)} %dynamic-slice_bitcast_fusion.5), channel_id=1, source_target_pairs={{0,1},{1,0},{2,3},{3,2},{4,5},{5,4},{6,7},{7,6},{8,9},{9,8},{10,11... | collective-permute-start | bytes 5308424 | tf_op jit(solution)/shard_map/ppermute | solution.py:58
  596.8 84.1 %collective-permute-start.85 = (bf16[16,96,768]{2,1,0:T(8,128)(2,1)}, bf16[16,96,768]{2,1,0:T(8,128)(2,1)}, u32[]{:S(2)}, u32[]{:S(2)}) collective-permute-start(bf16[16,96,768]{2,1,0:T(8,128)(2,1)} %dynamic-slice_bitcast_fusion), channel_id=1, source_target_pairs={{0,1},{1,0},{2,3},{3,2},{4,5},{5,4},{6,7},{7,6},{8,9},{9,8},{10,11... | collective-permute-start | bytes 7077896 | tf_op jit(solution)/shard_map/ppermute | solution.py:58
  609.1 81.5 %collective-permute-start.80 = (bf16[16,24,3072]{2,1,0:T(8,128)(2,1)}, bf16[16,24,3072]{2,1,0:T(8,128)(2,1)S(1)}, u32[]{:S(2)}, u32[]{:S(2)}) collective-permute-start(bf16[16,24,3072]{2,1,0:T(8,128)(2,1)} %dynamic-slice_bitcast_fusion.1), channel_id=1, source_target_pairs={{0,1},{1,0},{2,3},{3,2},{4,5},{5,4},{6,7},{7,6},{8,9},{9,8},{10,11... | collective-permute-start | bytes 7077896 | tf_op jit(solution)/shard_map/ppermute | solution.py:58
  684.8 43.2 %collective-permute-start.86 = (bf16[1,768,768]{2,1,0:T(8,128)(2,1)}, bf16[1,768,768]{2,1,0:T(8,128)(2,1)}, u32[]{:S(2)}, u32[]{:S(2)}) collective-permute-start(bf16[1,768,768]{2,1,0:T(8,128)(2,1)} %dynamic-slice_bitcast_fusion.6), channel_id=1, source_target_pairs={{0,16},{8,24},{16,0},{24,8},{1,17},{9,25},{17,1},{25,9},{2,18},{10... | collective-permute-start | bytes 3538952 | tf_op jit(solution)/shard_map/ppermute | solution.py:58
  722.6 51.7 %all-to-all-start.7 = ((bf16[8,3,192,128]{3,2,1,0:T(8,128)(2,1)}), bf16[8,3,192,128]{3,2,1,0:T(8,128)(2,1)S(1)}, u32[]{:S(2)}, u32[]{:S(2)}) async-start(bf16[8,3,192,128]{3,2,1,0:T(8,128)(2,1)} %copy.454), calls=%async_computation.7 | async-start | bytes 2359296 | tf_op jit(solution)/shard_map/all_to_all | solution.py:121
  (222 other events, 2096.3 us)
